TPU v7x, 32 devices: a whole 2x2x4 slice. The times are simulated.
32 devices in a mesh: dp: 16 (over z, y, x), mp: 2 (over core).
Axes of the slice: x: 2, y: 2, z: 4, core: 2. Of those that a mesh axis runs over, the one named last changes fastest.
Arguments:
- tokens: bfloat16 [11264, 1280], P('dp'), may hold values from -6 to 6
- cotangent: bfloat16 [11264, 1280], P('dp'), may hold values from -6 to 6
- segment_ids: int32 [704, 16], P('dp'), may hold values from 0 to 15, as said below
- valid_mask: int32 [704, 16], P('dp'), may hold values from 0 to 1, as said below
- frequency: int32 [704, 1], P('dp'), may hold values from 0 to 2
- query_weight: bfloat16 [1280, 1280], P('dp', 'mp'), may hold values from -0.15625 to 0.15625
- key_weight: bfloat16 [1280, 1280], P('dp', 'mp'), may hold values from -0.15625 to 0.15625
- value_weight: bfloat16 [1280, 1280], P('dp', 'mp'), may hold values from -0.15625 to 0.15625
- output_weight: bfloat16 [1280, 1280], P('mp', 'dp'), may hold values from -0.25 to 0.25
- attn_gain: bfloat16 [1280], P('dp'), may hold values from 0.5 to 1.5
- mlp_gain: bfloat16 [1280], P('dp'), may hold values from 0.5 to 1.5
- up_weight: bfloat16 [1280, 1280], P('dp', 'mp'), may hold values from -0.15625 to 0.15625
- up_bias: bfloat16 [1280], P('mp'), may hold values from -4 to 4
- down_weight: bfloat16 [1280, 1280], P('mp', 'dp'), may hold values from -0.25 to 0.25
- down_bias: bfloat16 [1280], P('dp'), may hold values from -4 to 4
Outputs:
- layer_out: bfloat16 [11264, 1280], P('dp')
- input_grad: float32 [11264, 1280], P('dp')
- query_grad: float32 [1280, 1280], P('dp', 'mp')
- key_grad: float32 [1280, 1280], P('dp', 'mp')
- value_grad: float32 [1280, 1280], P('dp', 'mp')
- output_grad: float32 [1280, 1280], P('mp', 'dp')
- attn_gain_grad: float32 [1280], P('dp')
- mlp_gain_grad: float32 [1280], P('dp')
- up_weight_grad: float32 [1280, 1280], P('dp', 'mp')
- up_bias_grad: float32 [1280], P('mp')
- down_weight_grad: float32 [1280, 1280], P('mp', 'dp')
- down_bias_grad: float32 [1280], P('dp')
Inputs may be any that keep to these rules, and one draw needn't show every extreme that they name: `segment_ids`: in each row the ids start at 0, never fall and rise by at most one from patch to patch; patches with equal ids belong to one packed series; some row gives every patch a series of its own. `valid_mask`: in each row a run of padding is followed by real patches up to the row's end; the last patch of every row is real. `frequency`: every class of 0 to 2 is given to some row.
All inputs are finite; a program needn't handle non-finite values.
Results may differ from a plain program's by a relative error of at most 0.011.
Values may be sent and summed in bfloat16 or wider, within the bound.
No kernel may reach another device: no remote copies, remote signals or barrier semaphores. Data moves between devices by JAX's collectives and lax.ppermute only.
A program may use at most 192 MiB of HBM per device.

v0:
```python
import math

import jax
import jax.numpy as jnp
from jax import lax
from jax.sharding import PartitionSpec as P

HD = 80
NCLASS = 3


def rms_scale(field):
    return lax.rsqrt(jnp.mean(field * field, axis=-1, keepdims=True) + 1e-06)


def rope_tables(length, width):
    half_width = width // 2
    rates = jnp.exp(-math.log(10000.0) * (2.0 * jnp.arange(half_width, dtype=jnp.float32) / width))
    angles = jnp.arange(length, dtype=jnp.float32)[:, None] * rates[None, :]
    return (jnp.cos(angles)[:, None, :], jnp.sin(angles)[:, None, :])


def rotate(field, cosine_table, sine_table):
    half_width = field.shape[-1] // 2
    first_half = field[..., :half_width]
    second_half = field[..., half_width:]
    return jnp.concatenate(
        [
            first_half * cosine_table - second_half * sine_table,
            second_half * cosine_table + first_half * sine_table,
        ],
        axis=-1,
    )


def allowed_pairs(segment_ids, valid_mask):
    places = jnp.arange(segment_ids.shape[1], dtype=jnp.int32)
    same_series = segment_ids[:, :, None] == segment_ids[:, None, :]
    causal = places[None, :, None] >= places[None, None, :]
    visible = (valid_mask[:, None, :] == 1) | (places[None, :, None] == places[None, None, :])
    return (same_series & causal & visible)[:, None, :, :]


def norm_back(field, scale, gain, grad):
    gain_grad = jnp.sum(grad * field * scale, axis=0)
    scaled = grad * gain
    inner = jnp.mean(scaled * field, axis=-1, keepdims=True)
    return (gain_grad, scale * scaled - field * (scale * scale * scale) * inner)


def local(
    tokens,
    cotangent,
    segment_ids,
    valid_mask,
    frequency,
    query_weight,
    key_weight,
    value_weight,
    output_weight,
    attn_gain,
    mlp_gain,
    up_weight,
    up_bias,
    down_weight,
    down_bias,
):
    block_rows = segment_ids.shape[0]
    patches = segment_ids.shape[1]
    token_count = block_rows * patches
    head_width = query_weight.shape[1]
    local_heads = head_width // HD
    shape_four = (block_rows, patches, local_heads, HD)
    score_root = math.sqrt(HD)
    member = (frequency == jnp.arange(NCLASS, dtype=jnp.int32)[None, :]).astype(jnp.int32)
    row_valid = jnp.sum(valid_mask, axis=1)
    local_counts = jnp.sum(member * row_valid[:, None], axis=0)
    class_count = lax.psum(local_counts, "dp")
    total = jnp.sum(class_count)
    row_count = jnp.sum(member * class_count[None, :], axis=1)
    row_weight = total.astype(jnp.float32) / (NCLASS * row_count.astype(jnp.float32))
    token_weight = (valid_mask.astype(jnp.float32) * row_weight[:, None]).reshape(token_count, 1)
    upstream = cotangent.astype(jnp.float32) * token_weight
    wq_full, wk_full, wv_full, wo_full, attn_gain_all = (
        lax.all_gather(query_weight, "dp", axis=0, tiled=True),
        lax.all_gather(key_weight, "dp", axis=0, tiled=True),
        lax.all_gather(value_weight, "dp", axis=0, tiled=True),
        lax.all_gather(output_weight, "dp", axis=1, tiled=True),
        lax.all_gather(attn_gain, "dp", axis=0, tiled=True),
    )
    up_full, down_full, mlp_gain_all, down_bias_all = (
        lax.all_gather(up_weight, "dp", axis=0, tiled=True),
        lax.all_gather(down_weight, "dp", axis=1, tiled=True),
        lax.all_gather(mlp_gain, "dp", axis=0, tiled=True),
        lax.all_gather(down_bias, "dp", axis=0, tiled=True),
    )
    gain_one = attn_gain_all.astype(jnp.float32)
    gain_two = mlp_gain_all.astype(jnp.float32)
    bias_two = down_bias_all.astype(jnp.float32)
    cosine_table, sine_table = rope_tables(patches, HD)
    allowed = allowed_pairs(segment_ids, valid_mask)
    inputs = tokens.astype(jnp.float32)
    scale_one = rms_scale(inputs)
    normed_one = (inputs * scale_one * gain_one).astype(jnp.bfloat16)
    query_pre = jnp.dot(normed_one, wq_full, preferred_element_type=jnp.float32)
    key_pre = jnp.dot(normed_one, wk_full, preferred_element_type=jnp.float32)
    value_pre = jnp.dot(normed_one, wv_full, preferred_element_type=jnp.float32)
    queries = rotate(query_pre.reshape(shape_four), cosine_table, sine_table).astype(jnp.bfloat16)
    key_rot = rotate(key_pre.reshape(shape_four), cosine_table, sine_table).astype(jnp.bfloat16)
    values = value_pre.reshape(shape_four).astype(jnp.bfloat16)
    scores = (
        jnp.einsum("rqhd,rkhd->rhqk", queries, key_rot, preferred_element_type=jnp.float32)
        / score_root
    )
    scores = jnp.where(allowed, scores, -1e30)
    exponent = jnp.exp(scores - jnp.max(scores, axis=-1, keepdims=True))
    softmax_out = exponent / jnp.sum(exponent, axis=-1, keepdims=True)
    softmax_low = softmax_out.astype(jnp.bfloat16)
    mixture = jnp.einsum("rhqk,rkhd->rqhd", softmax_low, values, preferred_element_type=jnp.float32)
    mixture = mixture.reshape(token_count, head_width).astype(jnp.bfloat16)
    attn_part = jnp.dot(mixture, wo_full, preferred_element_type=jnp.float32)
    hidden = inputs + lax.psum(attn_part, "mp")
    scale_two = rms_scale(hidden)
    normed_two = (hidden * scale_two * gain_two).astype(jnp.bfloat16)
    pre_act = jnp.dot(normed_two, up_full, preferred_element_type=jnp.float32) + up_bias.astype(
        jnp.float32
    )
    activated = jax.nn.silu(pre_act).astype(jnp.bfloat16)
    down_part = jnp.dot(activated, down_full, preferred_element_type=jnp.float32)
    down_half = lax.psum_scatter(
        down_part.astype(jnp.bfloat16), "mp", scatter_dimension=0, tiled=True
    ).astype(jnp.float32)
    share_rows = down_half.shape[0]
    first_row = lax.axis_index("mp") * share_rows
    hidden_half = lax.dynamic_slice_in_dim(hidden, first_row, share_rows, 0)
    out_half = (hidden_half + (down_half + bias_two)).astype(jnp.bfloat16)
    layer_out = lax.all_gather(out_half, "mp", axis=0, tiled=True)
    up_back, down_back = (
        lax.all_gather(up_weight, "dp", axis=0, tiled=True),
        lax.all_gather(down_weight, "dp", axis=1, tiled=True),
    )
    down_low = upstream.astype(jnp.bfloat16)
    down_bias_local = jnp.sum(down_low, axis=0, dtype=jnp.float32)
    down_weight_local = jnp.einsum(
        "nf,nd->fd", activated, down_low, preferred_element_type=jnp.float32
    )
    act_grad = jnp.einsum("nd,fd->nf", down_low, down_back, preferred_element_type=jnp.float32)
    sigmoid_val = jax.nn.sigmoid(pre_act)
    pre_grad = (act_grad * sigmoid_val * (1.0 + pre_act * (1.0 - sigmoid_val))).astype(jnp.bfloat16)
    up_bias_local = jnp.sum(pre_grad, axis=0, dtype=jnp.float32)
    up_weight_local = jnp.einsum(
        "nd,nf->df", normed_two, pre_grad, preferred_element_type=jnp.float32
    )
    normed_two_part = jnp.einsum("nf,df->nd", pre_grad, up_back, preferred_element_type=jnp.float32)
    normed_two_grad = lax.psum(normed_two_part, "mp")
    mlp_gain_local, hidden_from_norm = norm_back(hidden, scale_two, gain_two, normed_two_grad)
    hidden_grad = upstream + hidden_from_norm
    up_weight_grad, down_weight_grad, mlp_gain_grad, down_bias_grad = (
        lax.psum_scatter(up_weight_local, "dp", scatter_dimension=0, tiled=True),
        lax.psum_scatter(down_weight_local, "dp", scatter_dimension=1, tiled=True),
        lax.psum_scatter(mlp_gain_local, "dp", scatter_dimension=0, tiled=True),
        lax.psum_scatter(down_bias_local, "dp", scatter_dimension=0, tiled=True),
    )
    up_bias_grad = lax.psum(up_bias_local, "dp")
    wq_back, wk_back, wv_back, wo_back = (
        lax.all_gather(query_weight, "dp", axis=0, tiled=True),
        lax.all_gather(key_weight, "dp", axis=0, tiled=True),
        lax.all_gather(value_weight, "dp", axis=0, tiled=True),
        lax.all_gather(output_weight, "dp", axis=1, tiled=True),
    )
    attn_low = hidden_grad.astype(jnp.bfloat16)
    output_local = jnp.einsum("nc,nd->cd", mixture, attn_low, preferred_element_type=jnp.float32)
    mixture_grad = jnp.einsum("nd,cd->nc", attn_low, wo_back, preferred_element_type=jnp.float32)
    mixture_grad = mixture_grad.astype(jnp.bfloat16).reshape(shape_four)
    softmax_grad = jnp.einsum(
        "rqhd,rkhd->rhqk", mixture_grad, values, preferred_element_type=jnp.float32
    )
    value_pre_grad = jnp.einsum(
        "rhqk,rqhd->rkhd", softmax_low, mixture_grad, preferred_element_type=jnp.float32
    )
    value_pre_grad = value_pre_grad.reshape(token_count, head_width).astype(jnp.bfloat16)
    scores_grad = softmax_out * (
        softmax_grad - jnp.sum(softmax_out * softmax_grad, axis=-1, keepdims=True)
    )
    scores_grad = scores_grad.astype(jnp.bfloat16)
    query_rot_grad = (
        jnp.einsum("rhqk,rkhd->rqhd", scores_grad, key_rot, preferred_element_type=jnp.float32)
        / score_root
    )
    key_rot_grad = (
        jnp.einsum("rhqk,rqhd->rkhd", scores_grad, queries, preferred_element_type=jnp.float32)
        / score_root
    )
    query_pre_grad = (
        rotate(query_rot_grad, cosine_table, -sine_table)
        .reshape(token_count, head_width)
        .astype(jnp.bfloat16)
    )
    key_pre_grad = (
        rotate(key_rot_grad, cosine_table, -sine_table)
        .reshape(token_count, head_width)
        .astype(jnp.bfloat16)
    )
    query_local = jnp.einsum(
        "nd,nc->dc", normed_one, query_pre_grad, preferred_element_type=jnp.float32
    )
    key_local = jnp.einsum(
        "nd,nc->dc", normed_one, key_pre_grad, preferred_element_type=jnp.float32
    )
    value_local = jnp.einsum(
        "nd,nc->dc", normed_one, value_pre_grad, preferred_element_type=jnp.float32
    )
    normed_one_part = jnp.einsum(
        "nc,dc->nd", query_pre_grad, wq_back, preferred_element_type=jnp.float32
    )
    normed_one_part = normed_one_part + jnp.einsum(
        "nc,dc->nd", key_pre_grad, wk_back, preferred_element_type=jnp.float32
    )
    normed_one_part = normed_one_part + jnp.einsum(
        "nc,dc->nd", value_pre_grad, wv_back, preferred_element_type=jnp.float32
    )
    normed_one_grad = lax.psum(normed_one_part.astype(jnp.bfloat16), "mp").astype(jnp.float32)
    attn_gain_local, input_from_norm = norm_back(inputs, scale_one, gain_one, normed_one_grad)
    input_grad = hidden_grad + input_from_norm
    query_grad, key_grad, value_grad, output_grad, attn_gain_grad = (
        lax.psum_scatter(query_local, "dp", scatter_dimension=0, tiled=True),
        lax.psum_scatter(key_local, "dp", scatter_dimension=0, tiled=True),
        lax.psum_scatter(value_local, "dp", scatter_dimension=0, tiled=True),
        lax.psum_scatter(output_local, "dp", scatter_dimension=1, tiled=True),
        lax.psum_scatter(attn_gain_local, "dp", scatter_dimension=0, tiled=True),
    )
    return (
        layer_out,
        input_grad,
        query_grad,
        key_grad,
        value_grad,
        output_grad,
        attn_gain_grad,
        mlp_gain_grad,
        up_weight_grad,
        up_bias_grad,
        down_weight_grad,
        down_bias_grad,
    )


def solution(mesh):
    placed = (
        P("dp", None),
        P("dp", None),
        P("dp", None),
        P("dp", None),
        P("dp", None),
        P("dp", "mp"),
        P("dp", "mp"),
        P("dp", "mp"),
        P("mp", "dp"),
        P("dp"),
        P("dp"),
        P("dp", "mp"),
        P("mp"),
        P("mp", "dp"),
        P("dp"),
    )
    return jax.shard_map(
        local,
        mesh=mesh,
        in_specs=placed,
        out_specs=(
            P("dp", None),
            P("dp", None),
            P("dp", "mp"),
            P("dp", "mp"),
            P("dp", "mp"),
            P("mp", "dp"),
            P("dp"),
            P("dp"),
            P("dp", "mp"),
            P("mp"),
            P("mp", "dp"),
            P("dp"),
        ),
        check_vma=False,
    )
```

profile of v0, /device:TPU:0, one launch (start us, length us, event | category | flops | bytes accessed | tf_op | source)
XLA Modules:
  0.0 1046.9 jit_solution(10133037166161614814)
XLA Ops:
  17.3 78.9 %all-reduce.7 = (bf16[1280]{0:T(1024)(128)(2,1)S(1)}, bf16[1280]{0:T(1024)(128)(2,1)S(1)}, bf16[1280]{0:T(1024)(128)(2,1)S(1)}) all-reduce(bf16[1280]{0:T(1024)(128)(2,1)S(1)} %dynamic-update-slice, bf16[1280]{0:T(1024)(128)(2,1)S(1)} %dynamic-update-slice.1, bf16[1280]{0:T(1024)(128)(2,1)S(1)} %dynamic-update-slice.2), channel_id=1, replica_groups=mesh['dp'=16,'mp'=2] {'dp'}, use_global_device_ids=true, to_apply=%add | all-reduce | flops 3840 | bytes 15360
  103.6 28.0 %all-gather.10.cloned.1.call-done = bf16[1280,640]{1,0:T(8,128)(2,1)} async-done(((bf16[80,640]{1,0:T(8,128)(2,1)}), bf16[1280,640]{1,0:T(8,128)(2,1)}) %all-gather.10.cloned.1.call-update) | async-done | bytes 1638416 | tf_op jit(solution)/shard_map/all_gather | solution.py:85
  139.5 51.7 %all-gather.12.cloned.1.call-done = bf16[1280,640]{1,0:T(8,128)(2,1)} async-done(((bf16[80,640]{1,0:T(8,128)(2,1)}), bf16[1280,640]{1,0:T(8,128)(2,1)}) %all-gather.12.cloned.1.call-update) | async-done | bytes 1638416 | tf_op jit(solution)/shard_map/all_gather | solution.py:86
  199.2 8.9 fusion.54
  224.3 26.5 %all-gather.14.cloned.1.call-done = bf16[640,1280]{0,1:T(8,128)(2,1)} async-done(((bf16[640,80]{0,1:T(8,128)(2,1)}), bf16[640,1280]{0,1:T(8,128)(2,1)}) %all-gather.14.cloned.1.call-update) | async-done | bytes 1638416 | tf_op jit(solution)/shard_map/all_gather | solution.py:88
  250.8 5.1 fusion.58
  257.5 13.3 %psum.36 = s32[3]{0:T(128)S(1)} all-reduce(s32[3]{0:T(128)S(1)} %select_reduce_fusion.1), channel_id=1, replica_groups=mesh['dp'=16,'mp'=2] {'dp'}, use_global_device_ids=true, to_apply=%region_8.9 | all-reduce | flops 3 | bytes 24 | tf_op jit(solution)/shard_map/psum | solution.py:78
  272.3 6.7 all-reduce.12.cloned.1.call-done
  283.4 57.9 %all-gather.16.cloned.1.call-done = bf16[1280,640]{1,0:T(8,128)(2,1)} async-done(((bf16[80,640]{1,0:T(8,128)(2,1)}), bf16[1280,640]{1,0:T(8,128)(2,1)}) %all-gather.16.cloned.1.call-update) | async-done | bytes 1638416 | tf_op jit(solution)/shard_map/all_gather | solution.py:92
  341.3 5.4 fusion.42
  346.7 54.7 %all-gather.18.cloned.1.call-done = bf16[640,1280]{0,1:T(8,128)(2,1)} async-done(((bf16[640,80]{0,1:T(8,128)(2,1)}), bf16[640,1280]{0,1:T(8,128)(2,1)}) %all-gather.18.cloned.1.call-update) | async-done | bytes 1638416 | tf_op jit(solution)/shard_map/all_gather | solution.py:93
  410.3 5.0 convolution_convert_fusion
  415.4 18.0 %all-reduce.14.cloned.1.call-done = f32[704,1280]{1,0:T(8,128)} async-done(((f32[704,1280]{1,0:T(8,128)}), f32[704,1280]{1,0:T(8,128)}) %all-reduce.14.cloned.1.call-update) | async-done | bytes 3604496 | tf_op jit(solution)/shard_map/psum | solution.py:155
  449.5 6.1 multiply_reduce_fusion.3
  490.4 5.7 fusion.38
  496.2 6.1 fusion.41
  502.3 5.9 fusion.24
  525.1 77.4 %all-reduce.6 = (f32[1280]{0:T(1024)S(1)}, f32[1280]{0:T(1024)S(1)}, f32[640]{0:T(1024)}, f32[1280]{0:T(1024)S(1)}) all-reduce(f32[1280]{0:T(1024)S(1)} %get-tuple-element.14, f32[1280]{0:T(1024)S(1)} %get-tuple-element.12, f32[640]{0:T(1024)S(1)} %get-tuple-element.56, ...), channel_id=7, replica_groups=mesh['dp'=16,'mp'=2] {'dp'}, use_global_device_ids=true, to_apply=%region_21.22.clone | all-reduce | flops 4480 | bytes 35840
  604.3 5.4 fusion.3
  610.7 86.7 %reduce-scatter.18.cloned.1.call-done = f32[80,640]{1,0:T(8,128)} async-done(((f32[1280,640]{1,0:T(8,128)}), f32[80,640]{1,0:T(8,128)}) %reduce-scatter.18.cloned.1.call-update) | async-done | bytes 204816 | tf_op jit(solution)/shard_map/reduce_scatter | solution.py:159
  697.4 85.0 %reduce-scatter.16.cloned.1.call-done = f32[640,80]{0,1:T(8,128)} async-done(((f32[640,1280]{0,1:T(8,128)}), f32[640,80]{0,1:T(8,128)}) %reduce-scatter.16.cloned.1.call-update) | async-done | bytes 204816 | tf_op jit(solution)/shard_map/reduce_scatter | solution.py:229
  782.3 84.9 %reduce-scatter.14.cloned.1.call-done = f32[80,640]{1,0:T(8,128)} async-done(((f32[1280,640]{1,0:T(8,128)}), f32[80,640]{1,0:T(8,128)}) %reduce-scatter.14.cloned.1.call-update) | async-done | bytes 204816 | tf_op jit(solution)/shard_map/reduce_scatter | solution.py:228
  867.2 84.8 %reduce-scatter.12.cloned.1.call-done = f32[80,640]{1,0:T(8,128)} async-done(((f32[1280,640]{1,0:T(8,128)}), f32[80,640]{1,0:T(8,128)}) %reduce-scatter.12.cloned.1.call-update) | async-done | bytes 204816 | tf_op jit(solution)/shard_map/reduce_scatter | solution.py:227
  952.0 85.1 %reduce-scatter.10.cloned.1.call-done = f32[80,640]{1,0:T(8,128)} async-done(((f32[1280,640]{1,0:T(8,128)}), f32[80,640]{1,0:T(8,128)}) %reduce-scatter.10.cloned.1.call-update) | async-done | bytes 204816 | tf_op jit(solution)/shard_map/reduce_scatter | solution.py:226
  (164 shorter events, 136.9 us)
Async XLA Ops:
  7.2 90.2 %all-gather.8.cloned.1.call-start = ((), (), s32[]{:S(2)}) async-start(), calls=%async_computation.7 | async-start | bytes 1740800 | tf_op jit(solution)/shard_map/all_gather | solution.py:87
  7.9 123.6 %all-gather.10.cloned.1.call-start = ((), (), s32[]{:S(2)}) async-start(), calls=%async_computation.8 | async-start | bytes 1740800 | tf_op jit(solution)/shard_map/all_gather | solution.py:85
  8.7 182.6 %all-gather.12.cloned.1.call-start = ((), (), s32[]{:S(2)}) async-start(), calls=%async_computation.9 | async-start | bytes 1740800 | tf_op jit(solution)/shard_map/all_gather | solution.py:86
  9.4 241.4 %all-gather.14.cloned.1.call-start = ((), (), s32[]{:S(2)}) async-start(), calls=%async_computation.10 | async-start | bytes 1740800 | tf_op jit(solution)/shard_map/all_gather | solution.py:88
  10.0 269.1 %all-reduce.12.cloned.1.call-start = ((), (), s32[]{:S(2)}) async-start(), calls=%async_computation.11 | async-start | bytes 7208960 | tf_op jit(solution)/shard_map/psum | solution.py:122
  97.4 34.2 %copy-start.1 = (bf16[704,1280]{1,0:T(8,128)(2,1)S(1)}, bf16[704,1280]{1,0:T(8,128)(2,1)}, u32[]{:S(2)}) copy-start(bf16[704,1280]{1,0:T(8,128)(2,1)} %param.15) | copy-start | bytes 5406724
  255.9 16.1 %copy-start.19 = (bf16[640]{0:T(1024)(128)(2,1)S(1)}, bf16[640]{0:T(1024)(128)(2,1)}, u32[]{:S(2)}) copy-start(bf16[640]{0:T(1024)(128)(2,1)} %param.27) | copy-start | bytes 3844
  255.9 85.3 %all-gather.16.cloned.1.call-start = ((), (), s32[]{:S(2)}) async-start(), calls=%async_computation.12 | async-start | bytes 1740800 | tf_op jit(solution)/shard_map/all_gather | solution.py:92
  256.5 144.8 %all-gather.18.cloned.1.call-start = ((), (), s32[]{:S(2)}) async-start(), calls=%async_computation.13 | async-start | bytes 1740800 | tf_op jit(solution)/shard_map/all_gather | solution.py:93
  257.3 176.1 %all-reduce.14.cloned.1.call-start = ((), (), s32[]{:S(2)}) async-start(), calls=%async_computation.16 | async-start | bytes 7208960 | tf_op jit(solution)/shard_map/psum | solution.py:155
  401.3 5.5 copy-start.22
  410.3 77.1 %reduce-scatter.8.cloned.1.call-start = ((), (), s32[]{:S(2)}) async-start(), calls=%async_computation.14 | async-start | bytes 2703360 | tf_op jit(solution)/shard_map/reduce_scatter | solution.py:130
  415.3 107.0 %all-reduce.16.cloned.1.call-start = ((), (), s32[]{:S(2)}) async-start(), calls=%async_computation.17 | async-start | bytes 3604480 | tf_op jit(solution)/shard_map/psum | solution.py:222
  433.4 5.2 copy-start.3
  438.6 4.7 copy-start.21
  449.5 6.2 copy-start.12
  449.5 6.2 copy-start.15
  487.3 117.0 %all-gather.20.cloned.1.call-start = ((), (), s32[]{:S(2)}) async-start(), calls=%async_computation.15 | async-start | bytes 2703360 | tf_op jit(solution)/shard_map/all_gather | solution.py:137
  490.4 120.3 %reduce-scatter.20.cloned.1.call-start = ((), (), s32[]{:S(2)}) async-start(), calls=%async_computation.23 | async-start | bytes 3481600 | tf_op jit(solution)/shard_map/reduce_scatter | solution.py:160
  496.1 201.2 %reduce-scatter.18.cloned.1.call-start = ((), (), s32[]{:S(2)}) async-start(), calls=%async_computation.22 | async-start | bytes 3481600 | tf_op jit(solution)/shard_map/reduce_scatter | solution.py:159
  502.3 280.1 %reduce-scatter.16.cloned.1.call-start = ((), (), s32[]{:S(2)}) async-start(), calls=%async_computation.21 | async-start | bytes 3481600 | tf_op jit(solution)/shard_map/reduce_scatter | solution.py:229
  508.2 359.0 %reduce-scatter.14.cloned.1.call-start = ((), (), s32[]{:S(2)}) async-start(), calls=%async_computation.20 | async-start | bytes 3481600 | tf_op jit(solution)/shard_map/reduce_scatter | solution.py:228
  513.2 438.8 %reduce-scatter.12.cloned.1.call-start = ((), (), s32[]{:S(2)}) async-start(), calls=%async_computation.19 | async-start | bytes 3481600 | tf_op jit(solution)/shard_map/reduce_scatter | solution.py:227
  516.8 520.2 %reduce-scatter.10.cloned.1.call-start = ((), (), s32[]{:S(2)}) async-start(), calls=%async_computation.18 | async-start | bytes 3481600 | tf_op jit(solution)/shard_map/reduce_scatter | solution.py:226
  (18 other events, 39.6 us)
Sparse Core Ops, SparseCore 0:
  10.7 61.1 all-gather.7
  74.6 56.8 all-gather.9
  134.2 56.9 all-gather.11
  193.8 56.9 all-gather.13
  256.1 22.9 all-reduce.11
  282.0 59.2 all-gather.15
  344.3 56.9 all-gather.17
  410.4 22.9 all-reduce.13
  435.7 10.4 reduce-scatter.7
  487.4 21.9 all-reduce.15
  511.0 11.3 all-gather.19
  525.0 85.5 reduce-scatter.19
  613.6 83.7 reduce-scatter.17
  700.1 82.2 reduce-scatter.15
  785.1 82.1 reduce-scatter.13
  870.0 81.9 reduce-scatter.11
  954.7 82.2 reduce-scatter.9
where the time goes:
time: 1060 us; the launch traced here: 1050 us
  waiting for transfers between devices  675 us (64%)
  blocking collectives  170 us (16%)
  matrix products  87.1 us (8%)
  local copies, waits for them, and re-layouts  53.7 us (5%)
  other arithmetic  43.8 us (4%)
  between operations  16.8 us (2%)
    unnamed x2, blocking collectives  156 us
    reduce_scatter x1, waiting for transfers between devices, local(): lax.psum_scatter(up_weight_local, 'dp', scatter_dimension=0, tiled=True)  86.7 us
    reduce_scatter x1, waiting for transfers between devices, local(): lax.psum_scatter(query_local, 'dp', scatter_dimension=0, tiled=True)  85.1 us
    reduce_scatter x1, waiting for transfers between devices, local(): lax.psum_scatter(output_local, 'dp', scatter_dimension=1, tiled=True)  85 us
    reduce_scatter x1, waiting for transfers between devices, local(): lax.psum_scatter(value_local, 'dp', scatter_dimension=0, tiled=True)  84.9 us
    reduce_scatter x1, waiting for transfers between devices, local(): lax.psum_scatter(key_local, 'dp', scatter_dimension=0, tiled=True)  84.8 us
    all_gather x1, waiting for transfers between devices, local(): lax.all_gather(up_weight, 'dp', axis=0, tiled=True)  57.9 us
    all_gather x1, waiting for transfers between devices, local(): lax.all_gather(down_weight, 'dp', axis=1, tiled=True)  54.7 us
  transfers between devices with their start and end apart: 17, of which 13 were waited for; matrix products, arithmetic and copies ran while one was open for 15% of the time, Pallas kernels for 0%

commit v1 on v0

v1 whole, which is shorter than its diff:
```python
import functools
import math

import jax
import jax.numpy as jnp
from jax import lax
from jax.experimental import pallas as pl
from jax.experimental.pallas import tpu as pltpu
from jax.sharding import PartitionSpec as P

HD = 80
NCLASS = 3
EXTRA = 16
BF = jnp.bfloat16
F32 = jnp.float32


def pairs(move):
    out = []
    for z in range(4):
        for y in range(2):
            for x in range(2):
                a, b, c = move(z, y, x)
                out.append(((z * 2 + y) * 2 + x, (a * 2 + b) * 2 + c))
    return out


def over_x(field):
    return lax.ppermute(field, "dp", pairs(lambda z, y, x: (z, y, 1 - x)))


def over_y(field):
    return lax.ppermute(field, "dp", pairs(lambda z, y, x: (z, 1 - y, x)))


def up_z(field):
    return lax.ppermute(field, "dp", pairs(lambda z, y, x: ((z + 1) % 4, y, x)))


def over_mp(field):
    return lax.ppermute(field, "mp", [(0, 1), (1, 0)])


def gather_square(block):
    half = block.shape[0] // 2
    from_x = over_x(block)
    from_y = over_y(block)
    first = over_y(from_x[:half])
    second = over_x(from_y[half:])
    return jnp.stack([block, from_x, from_y, jnp.concatenate([first, second])])


def gather_line(block):
    parts = [block]
    for _ in range(3):
        parts.append(up_z(parts[-1]))
    return jnp.stack(parts)


def relative_of_absolute():
    me = lax.axis_index("dp")
    z, y, x = me // 4, (me // 2) % 2, me % 2
    absolute = jnp.arange(16, dtype=jnp.int32)
    za, ya, xa = absolute // 4, (absolute // 2) % 2, absolute % 2
    return (z - za + 4) % 4, (y ^ ya) * 2 + (x ^ xa)


def gather_rows(first, second):
    if lax.axis_size("dp") != 16:
        return tuple(lax.all_gather(f, "dp") for f in (first, second))
    line, square = relative_of_absolute()
    one = gather_line(gather_square(first).reshape(-1, first.shape[1]))
    one = one.reshape((16,) + first.shape)
    two = gather_square(gather_line(second).reshape(-1, second.shape[1]))
    two = two.reshape((16,) + second.shape)
    return jnp.take(one, line * 4 + square, axis=0), jnp.take(two, square * 4 + line, axis=0)


def scatter_square(parts):
    half = parts.shape[1] // 2
    diagonal = parts[3].astype(BF)
    via_x = over_x(diagonal[:half])
    via_y = over_y(diagonal[half:])
    to_y = jnp.concatenate([parts[2, :half] + via_x.astype(F32), parts[2, half:]]).astype(BF)
    to_x = jnp.concatenate([parts[1, :half], parts[1, half:] + via_y.astype(F32)]).astype(BF)
    return parts[0] + (over_x(to_x).astype(F32) + over_y(to_y).astype(F32))


def scatter_line(parts):
    total = parts[1]
    for k in (2, 3, 0):
        total = parts[k] + up_z(total.astype(BF)).astype(F32)
    return total


def scatter_rows(first, second):
    if lax.axis_size("dp") != 16:
        return tuple(
            lax.psum_scatter(f, "dp", scatter_dimension=0, tiled=False) for f in (first, second)
        )
    me = lax.axis_index("dp")
    z, y, x = me // 4, (me // 2) % 2, me % 2
    k = jnp.arange(4, dtype=jnp.int32)
    za = (z - k + 4) % 4
    sa = (y ^ (k // 2)) * 2 + (x ^ (k % 2))
    one = jnp.take(first, (za[:, None] * 4 + sa[None, :]).reshape(-1), axis=0)
    two = jnp.take(second, (sa[:, None] + za[None, :] * 4).reshape(-1), axis=0)
    cols = first.shape[2]
    one = scatter_line(one.reshape(4, -1, cols))
    one = scatter_square(one.reshape(4, -1, cols))
    two = scatter_square(two.reshape(4, -1, cols))
    two = scatter_line(two.reshape(4, -1, cols))
    return one, two


def rms_scale(field):
    return lax.rsqrt(jnp.mean(field * field, axis=-1, keepdims=True) + 1e-06)


def rope_tables(length, width):
    half_width = width // 2
    rates = jnp.exp(-math.log(10000.0) * (2.0 * jnp.arange(half_width, dtype=jnp.float32) / width))
    angles = jnp.arange(length, dtype=jnp.float32)[:, None] * rates[None, :]
    return (jnp.cos(angles)[:, None, :], jnp.sin(angles)[:, None, :])


def rotate(field, cosine_table, sine_table):
    half_width = field.shape[-1] // 2
    first_half = field[..., :half_width]
    second_half = field[..., half_width:]
    return jnp.concatenate(
        [
            first_half * cosine_table - second_half * sine_table,
            second_half * cosine_table + first_half * sine_table,
        ],
        axis=-1,
    )


def allowed_pairs(segment_ids, valid_mask):
    places = jnp.arange(segment_ids.shape[1], dtype=jnp.int32)
    same_series = segment_ids[:, :, None] == segment_ids[:, None, :]
    causal = places[None, :, None] >= places[None, None, :]
    visible = (valid_mask[:, None, :] == 1) | (places[None, :, None] == places[None, None, :])
    return (same_series & causal & visible)[:, None, :, :]


def norm_back(field, scale, gain, grad):
    gain_grad = jnp.sum(grad * field * scale, axis=0)
    scaled = grad * gain
    inner = jnp.mean(scaled * field, axis=-1, keepdims=True)
    return (gain_grad, scale * scaled - field * (scale * scale * scale) * inner)


def two_parts(vector):
    high = vector.astype(BF).astype(F32)
    return high, vector - high


def local(
    tokens,
    cotangent,
    segment_ids,
    valid_mask,
    frequency,
    query_weight,
    key_weight,
    value_weight,
    output_weight,
    attn_gain,
    mlp_gain,
    up_weight,
    up_bias,
    down_weight,
    down_bias,
):
    dp = lax.axis_size("dp")
    block_rows, patches = segment_ids.shape
    token_count = block_rows * patches
    share, head_width = query_weight.shape
    width = tokens.shape[1]
    local_heads = head_width // HD
    shape_four = (block_rows, patches, local_heads, HD)
    score_root = math.sqrt(HD)
    member = (frequency == jnp.arange(NCLASS, dtype=jnp.int32)[None, :]).astype(jnp.int32)
    row_valid = jnp.sum(valid_mask, axis=1)
    local_counts = jnp.sum(member * row_valid[:, None], axis=0)
    small = jnp.concatenate(
        [attn_gain, mlp_gain, down_bias, (local_counts // 16).astype(BF), (local_counts % 16).astype(BF)]
    )
    extra = jnp.pad(small[None, :], ((0, EXTRA - 1), (0, head_width - small.shape[0])))
    got_v, got_qk = gather_rows(
        value_weight, jnp.concatenate([query_weight, key_weight, extra])
    )
    wv_full = got_v.reshape(width, head_width)
    wq_full = got_qk[:, :share].reshape(width, head_width)
    wk_full = got_qk[:, share : 2 * share].reshape(width, head_width)
    small_all = got_qk[:, 2 * share, :]
    gain_one = small_all[:, :share].reshape(width).astype(F32)
    gain_two = small_all[:, share : 2 * share].reshape(width).astype(F32)
    bias_two = small_all[:, 2 * share : 3 * share].reshape(width).astype(F32)
    counts = small_all[:, 3 * share : 3 * share + 2 * NCLASS].astype(F32)
    counts = jnp.sum(counts, axis=0)
    class_count = (counts[:NCLASS] * 16.0 + counts[NCLASS:]).astype(jnp.int32)

    second_in = (output_weight.T, up_weight, down_weight.T)
    got_qk, second_in = lax.optimization_barrier((got_qk, second_in))
    wo_t, up_rows, down_t = second_in
    got_o, got_ud = gather_rows(wo_t, jnp.concatenate([up_rows, down_t]))
    wo_t = got_o.reshape(width, head_width)
    up_full = got_ud[:, :share].reshape(width, head_width)
    down_t = got_ud[:, share:].reshape(width, head_width)

    total = jnp.sum(class_count)
    row_count = jnp.sum(member * class_count[None, :], axis=1)
    row_weight = total.astype(jnp.float32) / (NCLASS * row_count.astype(jnp.float32))
    token_weight = (valid_mask.astype(jnp.float32) * row_weight[:, None]).reshape(token_count, 1)
    upstream = cotangent.astype(jnp.float32) * token_weight

    cosine_table, sine_table = rope_tables(patches, HD)
    allowed = allowed_pairs(segment_ids, valid_mask)
    inputs = tokens.astype(jnp.float32)
    scale_one = rms_scale(inputs)
    normed_one = (inputs * scale_one * gain_one).astype(jnp.bfloat16)
    query_pre = jnp.dot(normed_one, wq_full, preferred_element_type=jnp.float32)
    key_pre = jnp.dot(normed_one, wk_full, preferred_element_type=jnp.float32)
    value_pre = jnp.dot(normed_one, wv_full, preferred_element_type=jnp.float32)
    queries = rotate(query_pre.reshape(shape_four), cosine_table, sine_table).astype(jnp.bfloat16)
    key_rot = rotate(key_pre.reshape(shape_four), cosine_table, sine_table).astype(jnp.bfloat16)
    values = value_pre.reshape(shape_four).astype(jnp.bfloat16)
    scores = (
        jnp.einsum("rqhd,rkhd->rhqk", queries, key_rot, preferred_element_type=jnp.float32)
        / score_root
    )
    scores = jnp.where(allowed, scores, -1e30)
    exponent = jnp.exp(scores - jnp.max(scores, axis=-1, keepdims=True))
    softmax_out = exponent / jnp.sum(exponent, axis=-1, keepdims=True)
    softmax_low = softmax_out.astype(jnp.bfloat16)
    mixture = jnp.einsum("rhqk,rkhd->rqhd", softmax_low, values, preferred_element_type=jnp.float32)
    mixture = mixture.reshape(token_count, head_width).astype(jnp.bfloat16)
    attn_part = jnp.einsum("nc,dc->nd", mixture, wo_t, preferred_element_type=jnp.float32).astype(BF)
    hidden = inputs + (attn_part.astype(F32) + over_mp(attn_part).astype(F32))
    scale_two = rms_scale(hidden)
    normed_two = (hidden * scale_two * gain_two).astype(jnp.bfloat16)
    pre_act = jnp.dot(normed_two, up_full, preferred_element_type=jnp.float32) + up_bias.astype(
        jnp.float32
    )
    activated = jax.nn.silu(pre_act).astype(jnp.bfloat16)
    down_part = jnp.einsum("nf,df->nd", activated, down_t, preferred_element_type=jnp.float32)
    down_part = down_part.astype(BF)
    layer_out = hidden + (down_part.astype(F32) + over_mp(down_part).astype(F32) + bias_two)
    layer_out = layer_out.astype(BF)

    down_low = upstream.astype(jnp.bfloat16)
    down_bias_local = jnp.sum(down_low, axis=0, dtype=jnp.float32)
    down_weight_local = jnp.einsum(
        "nd,nf->df", down_low, activated, preferred_element_type=jnp.float32
    )
    act_grad = jnp.dot(down_low, down_t, preferred_element_type=jnp.float32)
    sigmoid_val = jax.nn.sigmoid(pre_act)
    pre_grad = (act_grad * sigmoid_val * (1.0 + pre_act * (1.0 - sigmoid_val))).astype(jnp.bfloat16)
    up_bias_local = jnp.sum(pre_grad, axis=0, dtype=jnp.float32)
    up_weight_local = jnp.einsum(
        "nd,nf->df", normed_two, pre_grad, preferred_element_type=jnp.float32
    )
    normed_two_part = jnp.einsum(
        "nf,df->nd", pre_grad, up_full, preferred_element_type=jnp.float32
    ).astype(BF)
    normed_two_grad = normed_two_part.astype(F32) + over_mp(normed_two_part).astype(F32)
    mlp_gain_local, hidden_from_norm = norm_back(hidden, scale_two, gain_two, normed_two_grad)
    hidden_grad = upstream + hidden_from_norm

    attn_low = hidden_grad.astype(jnp.bfloat16)
    output_local = jnp.einsum("nd,nc->dc", attn_low, mixture, preferred_element_type=jnp.float32)

    blocks = lambda grad: grad.reshape(dp, share, head_width)
    bias_rows = jnp.stack([jnp.broadcast_to(v, (dp, head_width)) for v in two_parts(up_bias_local)], 1)
    vectors = [v.reshape(dp, share) for f in (mlp_gain_local, down_bias_local) for v in two_parts(f)]
    vector_row = jnp.concatenate(vectors, 1)
    vector_row = jnp.pad(vector_row, ((0, 0), (0, head_width - vector_row.shape[1])))
    rows = jnp.concatenate([bias_rows, vector_row[:, None]], 1)
    rows = jnp.pad(rows, ((0, 0), (0, EXTRA - 3), (0, 0)))
    sum_o, sum_ud = scatter_rows(
        blocks(output_local),
        jnp.concatenate([blocks(up_weight_local), blocks(down_weight_local), rows], 1),
    )
    output_grad = sum_o.T
    up_weight_grad = sum_ud[:share]
    down_weight_grad = sum_ud[share : 2 * share].T
    up_bias_grad = sum_ud[2 * share] + sum_ud[2 * share + 1]
    vec = sum_ud[2 * share + 2]
    mlp_gain_grad = vec[:share] + vec[share : 2 * share]
    down_bias_grad = vec[2 * share : 3 * share] + vec[3 * share : 4 * share]

    mixture_grad = jnp.dot(attn_low, wo_t, preferred_element_type=jnp.float32)
    mixture_grad = mixture_grad.astype(jnp.bfloat16).reshape(shape_four)
    softmax_grad = jnp.einsum(
        "rqhd,rkhd->rhqk", mixture_grad, values, preferred_element_type=jnp.float32
    )
    value_pre_grad = jnp.einsum(
        "rhqk,rqhd->rkhd", softmax_low, mixture_grad, preferred_element_type=jnp.float32
    )
    value_pre_grad = value_pre_grad.reshape(token_count, head_width).astype(jnp.bfloat16)
    scores_grad = softmax_out * (
        softmax_grad - jnp.sum(softmax_out * softmax_grad, axis=-1, keepdims=True)
    )
    scores_grad = scores_grad.astype(jnp.bfloat16)
    query_rot_grad = (
        jnp.einsum("rhqk,rkhd->rqhd", scores_grad, key_rot, preferred_element_type=jnp.float32)
        / score_root
    )
    key_rot_grad = (
        jnp.einsum("rhqk,rqhd->rkhd", scores_grad, queries, preferred_element_type=jnp.float32)
        / score_root
    )
    query_pre_grad = (
        rotate(query_rot_grad, cosine_table, -sine_table)
        .reshape(token_count, head_width)
        .astype(jnp.bfloat16)
    )
    key_pre_grad = (
        rotate(key_rot_grad, cosine_table, -sine_table)
        .reshape(token_count, head_width)
        .astype(jnp.bfloat16)
    )
    query_local = jnp.einsum(
        "nd,nc->dc", normed_one, query_pre_grad, preferred_element_type=jnp.float32
    )
    key_local = jnp.einsum(
        "nd,nc->dc", normed_one, key_pre_grad, preferred_element_type=jnp.float32
    )
    value_local = jnp.einsum(
        "nd,nc->dc", normed_one, value_pre_grad, preferred_element_type=jnp.float32
    )
    normed_one_part = jnp.einsum(
        "nc,dc->nd", query_pre_grad, wq_full, preferred_element_type=jnp.float32
    )
    normed_one_part = normed_one_part + jnp.einsum(
        "nc,dc->nd", key_pre_grad, wk_full, preferred_element_type=jnp.float32
    )
    normed_one_part = normed_one_part + jnp.einsum(
        "nc,dc->nd", value_pre_grad, wv_full, preferred_element_type=jnp.float32
    )
    normed_one_part = normed_one_part.astype(BF)
    normed_one_grad = normed_one_part.astype(F32) + over_mp(normed_one_part).astype(F32)
    attn_gain_local, input_from_norm = norm_back(inputs, scale_one, gain_one, normed_one_grad)
    input_grad = hidden_grad + input_from_norm
    gain_row = jnp.concatenate([v.reshape(dp, share) for v in two_parts(attn_gain_local)], 1)
    gain_row = jnp.pad(gain_row, ((0, 0), (0, head_width - gain_row.shape[1])))[:, None]
    gain_row = jnp.pad(gain_row, ((0, 0), (0, EXTRA - 1), (0, 0)))
    sum_v, sum_qk = scatter_rows(
        blocks(value_local),
        jnp.concatenate([blocks(query_local), blocks(key_local), gain_row], 1),
    )
    query_grad = sum_qk[:share]
    key_grad = sum_qk[share : 2 * share]
    value_grad = sum_v
    attn_gain_grad = sum_qk[2 * share, :share] + sum_qk[2 * share, share : 2 * share]
    return (
        layer_out,
        input_grad,
        query_grad,
        key_grad,
        value_grad,
        output_grad,
        attn_gain_grad,
        mlp_gain_grad,
        up_weight_grad,
        up_bias_grad,
        down_weight_grad,
        down_bias_grad,
    )


def solution(mesh):
    rows = P("dp", None)
    wide = P("dp", "mp")
    tall = P("mp", "dp")
    return jax.shard_map(
        local,
        mesh=mesh,
        in_specs=(rows,) * 5
        + (wide, wide, wide, tall, P("dp"), P("dp"), wide, P("mp"), tall, P("dp")),
        out_specs=(rows, rows, wide, wide, wide, tall, P("dp"), P("dp"), wide, P("mp"), tall, P("dp")),
        check_vma=False,
    )
```

time: 1060 us -> 530 us (0.50)
  waiting for transfers between devices: 675 us -> 146 us
  blocking collectives: 170 us -> 0 us
  local copies, waits for them, and re-layouts: 53.7 us -> 136 us
  other arithmetic: 43.8 us -> 112 us
  starting transfers between devices: 0.94 us -> 49.3 us
  between operations: 16.8 us -> 2.6 us
  matrix products: 87.1 us -> 75.6 us
    reduce_scatter x7 -> x0, waiting for transfers between devices: 427 us -> none  [the longest x1 86.7 us: local(): lax.psum_scatter(up_weight_local, 'dp', scatter_dimension=0, tiled=True)]
    all_gather x7 -> x0, waiting for transfers between devices: 219 us -> none  [the longest x1 57.9 us: local(): lax.all_gather(up_weight, 'dp', axis=0, tiled=True)]
    unnamed x2 -> x0, blocking collectives: 156 us -> none
    ppermute x0 -> x60, waiting for transfers between devices: none -> 146 us  [the longest x24 87.6 us: up_z(): return lax.ppermute(field, 'dp', pairs(lambda z, y, x: ((z + 1) % 4, y, x)))]
    ppermute x0 -> x60, starting transfers between devices: none -> 49.3 us  [the longest x16 19.2 us: over_y(): return lax.ppermute(field, 'dp', pairs(lambda z, y, x: (z, 1 - y, x)))]
    gather x0 -> x8, local copies, waits for them, and re-layouts: none -> 38.6 us  [the longest x2 14.3 us: scatter_rows(): two = jnp.take(second, (sa[:, None] + za[None, :] * 4).reshape(-1), axis=0)]
    another operation x2 -> x26, other arithmetic: 7.83 us -> 33.5 us
    psum x3 -> x0, waiting for transfers between devices: 24.8 us -> none  [the longest x1 18 us: local(): normed_two_grad = lax.psum(normed_two_part, 'mp')]
  transfers between devices with their start and end apart: 17 -> 60, of which waited for: 13 -> 31; matrix products, arithmetic and copies ran while one was open for 15% -> 34% of each run, Pallas kernels for 0% -> 0%
where the time goes in v1:
time: 530 us; the launch traced here: 521 us
  waiting for transfers between devices  146 us (28%)
  local copies, waits for them, and re-layouts  136 us (26%)
  other arithmetic  112 us (21%)
  matrix products  75.6 us (14%)
  starting transfers between devices  49.3 us (9%)
    ppermute x24, waiting for transfers between devices, up_z(): return lax.ppermute(field, 'dp', pairs(lambda z, y, x: ((z + 1) % 4, y, x)))  87.6 us
    ppermute x16, waiting for transfers between devices, over_x(): return lax.ppermute(field, 'dp', pairs(lambda z, y, x: (z, y, 1 - x)))  35.5 us
    ppermute x16, waiting for transfers between devices, over_y(): return lax.ppermute(field, 'dp', pairs(lambda z, y, x: (z, 1 - y, x)))  22.4 us
    ppermute x16, starting transfers between devices, over_y(): return lax.ppermute(field, 'dp', pairs(lambda z, y, x: (z, 1 - y, x)))  19.2 us
    ppermute x16, starting transfers between devices, over_x(): return lax.ppermute(field, 'dp', pairs(lambda z, y, x: (z, y, 1 - x)))  18 us
    another operation x13, other arithmetic  17.9 us
    convert_element_type x3, local copies, waits for them, and re-layouts, local(): mixture = mixture.reshape(token_count, head_width).astype(jnp.bfloat16)  15.9 us
    gather x2, local copies, waits for them, and re-layouts, scatter_rows(): two = jnp.take(second, (sa[:, None] + za[None, :] * 4).reshape(-1), axis=0)  14.3 us
  transfers between devices with their start and end apart: 60, of which 31 were waited for; matrix products, arithmetic and copies ran while one was open for 34% of the time, Pallas kernels for 0%

profile of v1, /device:TPU:0, one launch (start us, length us, event | category | flops | bytes accessed | tf_op | source)
XLA Modules:
  0.0 520.8 jit_solution(17820161507863094995)
XLA Ops:
  20.8 5.3 %collective-permute-done.1 = bf16[176,640]{1,0:T(8,128)(2,1)S(1)} collective-permute-done((bf16[176,640]{1,0:T(8,128)(2,1)S(1)}, bf16[176,640]{1,0:T(8,128)(2,1)S(1)}, u32[]{:S(2)}, u32[]{:S(2)}) %collective-permute-start.1) | collective-permute-done | bytes 225312 | tf_op jit(solution)/shard_map/ppermute | solution.py:37
  26.3 10.1 %collective-permute-done.2 = bf16[176,640]{1,0:T(8,128)(2,1)S(1)} collective-permute-done((bf16[176,640]{1,0:T(8,128)(2,1)S(1)}, bf16[176,640]{1,0:T(8,128)(2,1)S(1)}, u32[]{:S(2)}, u32[]{:S(2)}) %collective-permute-start.2) | collective-permute-done | bytes 225312 | tf_op jit(solution)/shard_map/ppermute | solution.py:37
  45.4 9.1 %collective-permute-done.12 = bf16[320,640]{1,0:T(8,128)(2,1)S(1)} collective-permute-done((bf16[320,640]{1,0:T(8,128)(2,1)S(1)}, bf16[320,640]{1,0:T(8,128)(2,1)S(1)}, u32[]{:S(2)}, u32[]{:S(2)}) %collective-permute-start.12) | collective-permute-done | bytes 409632 | tf_op jit(solution)/shard_map/ppermute | solution.py:37
  72.4 5.0 gather_fusion
  96.4 5.6 %fusion.119 = f32[44,16,8,80]{3,1,2,0:T(8,128)} fusion(bf16[44,16,1280,1]{2,1,3,0:T(8,128)(2,1)} %bitcast.287, bf16[8,80,1280,1]{2,1,0,3:T(8,128)(2,1)} %bitcast.299), kind=kOutput, calls=%fused_computation.343 | convolution fusion | flops 1153433600 | bytes 5242880 | tf_op jit(solution)/shard_map/dot_general | solution.py:226
  116.7 5.0 collective-permute-done.18
  178.2 7.3 %collective-permute-done.27 = bf16[320,640]{1,0:T(8,128)(2,1)} collective-permute-done((bf16[320,640]{1,0:T(8,128)(2,1)}, bf16[320,640]{1,0:T(8,128)(2,1)}, u32[]{:S(2)}, u32[]{:S(2)}) %collective-permute-start.27) | collective-permute-done | bytes 409632 | tf_op jit(solution)/shard_map/ppermute | solution.py:33
  217.0 10.9 %reshape.790 = bf16[704,640,1]{1,0,2:T(8,128)(2,1)} reshape(bf16[44,16,8,80]{3,2,1,0:T(8,128)(2,1)} %copy.80) | data formatting | bytes 1802240 | tf_op jit(solution)/shard_map/convert_element_type | solution.py:240
  243.0 5.4 %convert_bitcast_fusion = (bf16[1280,704]{0,1:T(8,128)(2,1)}, f32[704,1280]{1,0:T(8,128)S(1)}, bf16[704,1280]{1,0:T(8,128)(2,1)}, f32[1280]{0:T(1024)S(1)}) fusion(f32[704]{0:T(1024)S(1)} %broadcast_multiply_fusion.1, f32[704,1280]{1,0:T(8,128)S(1)} %copy-done.2, f32[704]{0:T(1024)S(1)} %get-tuple-element.110, f32[1280]{0:T(1024)S(1)} %reshape.699, ...), kind=kLoop, calls=%fused_computation.114 | loop fusion | flops 18922240 | bytes 19851264 | tf_op jit(solution)/shard_map/nd,nc->dc/dot_general | solution.py:274
  293.2 5.2 fusion.124
  303.0 5.2 %fusion.123 = f32[16,80,640]{2,1,0:T(8,128)} fusion(bf16[16,80,704]{2,1,0:T(8,128)(2,1)} %bitcast.283, bf16[704,640,1]{1,0,2:T(8,128)(2,1)} %reshape.789), kind=kOutput, calls=%fused_computation.347 | convolution fusion | flops 1153433600 | bytes 5980160 | tf_op jit(solution)/shard_map/nd,nc->dc/dot_general | solution.py:332
  312.8 5.2 %broadcast_select_fusion.4 = (f32[16,80,640]{2,1,0:T(8,128)S(1)}, f32[16,80,640]{2,1,0:T(8,128)}) fusion(f32[16,80,640]{2,1,0:T(8,128)} %gather_fusion.6, pred[16]{0:T(512)(128)(4,1)S(1)} %copy-done.61, f32[16,80,640]{2,1,0:T(8,128)} %gather_fusion.5), kind=kLoop, calls=%fused_computation.78 | loop fusion | flops 1638400 | bytes 13107216 | tf_op jit(solution)/shard_map/jit(_take)/select_n | solution.py:106
  344.8 5.4 %fusion.121 = f32[16,80,640]{2,1,0:T(8,128)} fusion(bf16[16,80,704]{2,1,0:T(8,128)(2,1)} %bitcast.284, bf16[704,640,1]{1,0,2:T(8,128)(2,1)} %reshape.787), kind=kOutput, calls=%fused_computation.345 | convolution fusion | flops 1153433600 | bytes 5980160 | tf_op jit(solution)/shard_map/nd,nc->dc/dot_general | solution.py:326
  355.2 6.0 %collective-permute-done.39 = bf16[320,640]{1,0:T(8,128)(2,1)S(1)} collective-permute-done((bf16[320,640]{1,0:T(8,128)(2,1)S(1)}, bf16[320,640]{1,0:T(8,128)(2,1)S(1)}, u32[]{:S(2)}, u32[]{:S(2)}) %collective-permute-start.39) | collective-permute-done | bytes 409632 | tf_op jit(solution)/shard_map/ppermute | solution.py:37
  362.0 7.9 %collective-permute-done.47 = bf16[320,640]{1,0:T(8,128)(2,1)S(1)} collective-permute-done((bf16[320,640]{1,0:T(8,128)(2,1)S(1)}, bf16[320,640]{1,0:T(8,128)(2,1)S(1)}, u32[]{:S(2)}, u32[]{:S(2)}) %collective-permute-start.47) | collective-permute-done | bytes 409632 | tf_op jit(solution)/shard_map/ppermute | solution.py:37
  374.0 7.2 %gather_fusion.7 = f32[16,176,640]{2,1,0:T(8,128)} fusion(f32[16,176,640]{2,1,0:T(8,128)} %pad_maximum_fusion, s32[1024]{0:T(1024)} %get-tuple-element.133), kind=kCustom, calls=%fused_computation.4.clone | custom fusion | bytes 14417984 | tf_op jit(solution)/shard_map/jit(_take)/gather | solution.py:107
  382.6 5.1 collective-permute-done.48
  411.4 5.1 select_maximum_fusion
  416.5 7.1 %gather_fusion.4 = f32[16,176,640]{2,1,0:T(8,128)} fusion(f32[16,176,640]{2,1,0:T(8,128)} %select_maximum_fusion, s32[1024]{0:T(1024)} %get-tuple-element.133), kind=kCustom, calls=%fused_computation.1.clone | custom fusion | bytes 14417984 | tf_op jit(solution)/shard_map/jit(_take)/gather | solution.py:107
  423.6 7.6 %fusion.103 = (bf16[16,176,640]{2,1,0:T(8,128)(2,1)}, f32[16,176,640]{2,1,0:T(8,128)S(1)}, bf16[16,176,640]{2,1,0:T(8,128)(2,1)S(1)}, f32[16,176,640]{2,1,0:T(8,128)S(1)}) fusion(f32[16,176,640]{2,1,0:T(8,128)} %gather_fusion.7, pred[16]{0:T(512)(128)(4,1)S(1)} %copy-done.60, f32[16,176,640]{2,1,0:T(8,128)} %gather_fusion.4), kind=kLoop, calls=%fused_computation.327 | loop fusion | flops 7208960 | bytes 36044816 | tf_op jit(solution)/shard_map/convert.12
  438.8 8.2 %collective-permute-done.53 = bf16[352,640]{1,0:T(8,128)(2,1)} collective-permute-done((bf16[352,640]{1,0:T(8,128)(2,1)}, bf16[352,640]{1,0:T(8,128)(2,1)}, u32[]{:S(2)}, u32[]{:S(2)}) %collective-permute-start.53) | collective-permute-done | bytes 450592 | tf_op jit(solution)/shard_map/ppermute | solution.py:33
  465.6 11.8 %collective-permute-done.54 = bf16[704,640]{1,0:T(8,128)(2,1)S(1)} collective-permute-done((bf16[704,640]{1,0:T(8,128)(2,1)S(1)}, bf16[704,640]{1,0:T(8,128)(2,1)S(1)}, u32[]{:S(2)}, u32[]{:S(2)}) %collective-permute-start.54) | collective-permute-done | bytes 901152 | tf_op jit(solution)/shard_map/ppermute | solution.py:29
  477.8 15.0 %collective-permute-done.33 = bf16[704,640]{1,0:T(8,128)(2,1)S(1)} collective-permute-done((bf16[704,640]{1,0:T(8,128)(2,1)S(1)}, bf16[704,640]{1,0:T(8,128)(2,1)S(1)}, u32[]{:S(2)}, u32[]{:S(2)}) %collective-permute-start.33) | collective-permute-done | bytes 901152 | tf_op jit(solution)/shard_map/ppermute | solution.py:29
  493.3 8.2 %collective-permute-done.36 = bf16[176,640]{1,0:T(8,128)(2,1)S(1)} collective-permute-done((bf16[176,640]{1,0:T(8,128)(2,1)S(1)}, bf16[176,640]{1,0:T(8,128)(2,1)S(1)}, u32[]{:S(2)}, u32[]{:S(2)}) %collective-permute-start.36) | collective-permute-done | bytes 225312 | tf_op jit(solution)/shard_map/ppermute | solution.py:37
  (443 shorter events, 344.2 us)
Async XLA Ops:
  0.7 18.4 %collective-permute-start.8 = (bf16[80,640]{1,0:T(8,128)(2,1)}, bf16[80,640]{1,0:T(8,128)(2,1)S(1)}, u32[]{:S(2)}, u32[]{:S(2)}) collective-permute-start(bf16[80,640]{1,0:T(8,128)(2,1)} %param.28), channel_id=1, source_target_pairs={{0,4},{2,6},{4,0},{6,2},{8,12},{10,14},{12,8},{14,10},{16,20},{18,... | collective-permute-start | bytes 307208 | tf_op jit(solution)/shard_map/ppermute | solution.py:33
  3.7 15.9 %collective-permute-start.7 = (bf16[80,640]{1,0:T(8,128)(2,1)}, bf16[80,640]{1,0:T(8,128)(2,1)S(1)}, u32[]{:S(2)}, u32[]{:S(2)}) collective-permute-start(bf16[80,640]{1,0:T(8,128)(2,1)} %param.28), channel_id=1, source_target_pairs={{0,2},{2,0},{4,6},{6,4},{8,10},{10,8},{12,14},{14,12},{16,18},{18,... | collective-permute-start | bytes 307208 | tf_op jit(solution)/shard_map/ppermute | solution.py:29
  26.3 16.6 %collective-permute-start.11 = (bf16[320,640]{1,0:T(8,128)(2,1)S(1)}, bf16[320,640]{1,0:T(8,128)(2,1)S(1)}, u32[]{:S(2)}, u32[]{:S(2)}) collective-permute-start(bf16[320,640]{1,0:T(8,128)(2,1)S(1)} %bitcast.290), channel_id=1, source_target_pairs={{0,8},{2,10},{4,12},{6,14},{8,16},{10,18},{12,20},{14,22},{16,24},... | collective-permute-start | bytes 1228808 | tf_op jit(solution)/shard_map/ppermute | solution.py:37
  36.5 18.5 %collective-permute-start.3 = (bf16[704,640]{1,0:T(8,128)(2,1)S(1)}, bf16[704,640]{1,0:T(8,128)(2,1)S(1)}, u32[]{:S(2)}, u32[]{:S(2)}) collective-permute-start(bf16[704,640]{1,0:T(8,128)(2,1)S(1)} %bitcast.276), channel_id=1, source_target_pairs={{0,2},{2,0},{4,6},{6,4},{8,10},{10,8},{12,14},{14,12},{16,18},{18,... | collective-permute-start | bytes 2703368 | tf_op jit(solution)/shard_map/ppermute | solution.py:29
  37.1 21.2 %collective-permute-start.4 = (bf16[704,640]{1,0:T(8,128)(2,1)S(1)}, bf16[704,640]{1,0:T(8,128)(2,1)S(1)}, u32[]{:S(2)}, u32[]{:S(2)}) collective-permute-start(bf16[704,640]{1,0:T(8,128)(2,1)S(1)} %bitcast.277), channel_id=1, source_target_pairs={{0,4},{2,6},{4,0},{6,2},{8,12},{10,14},{12,8},{14,10},{16,20},{18,... | collective-permute-start | bytes 2703368 | tf_op jit(solution)/shard_map/ppermute | solution.py:33
  85.5 26.8 %collective-permute-start.22 = (bf16[160,640]{1,0:T(8,128)(2,1)}, bf16[160,640]{1,0:T(8,128)(2,1)}, u32[]{:S(2)}, u32[]{:S(2)}) collective-permute-start(bf16[160,640]{1,0:T(8,128)(2,1)} %constant_dynamic-update-slice_fusion), channel_id=1, source_target_pairs={{0,8},{2,10},{4,12},{6,14},{8,16},{10,18},{12,20},{14,22},{16,24},... | collective-permute-start | bytes 614408 | tf_op jit(solution)/shard_map/ppermute | solution.py:37
  112.3 14.7 %collective-permute-start.23 = (bf16[160,640]{1,0:T(8,128)(2,1)}, bf16[160,640]{1,0:T(8,128)(2,1)S(1)}, u32[]{:S(2)}, u32[]{:S(2)}) collective-permute-start(bf16[160,640]{1,0:T(8,128)(2,1)} %collective-permute-done.22), channel_id=1, source_target_pairs={{0,8},{2,10},{4,12},{6,14},{8,16},{10,18},{12,20},{14,22},{16,24},... | collective-permute-start | bytes 614408 | tf_op jit(solution)/shard_map/ppermute | solution.py:37
  138.9 32.6 %collective-permute-start.25 = (bf16[640,640]{1,0:T(8,128)(2,1)}, bf16[640,640]{1,0:T(8,128)(2,1)}, u32[]{:S(2)}, u32[]{:S(2)}) collective-permute-start(bf16[640,640]{1,0:T(8,128)(2,1)} %bitcast.58), channel_id=1, source_target_pairs={{0,2},{2,0},{4,6},{6,4},{8,10},{10,8},{12,14},{14,12},{16,18},{18,... | collective-permute-start | bytes 2457608 | tf_op jit(solution)/shard_map/ppermute | solution.py:29
  140.3 34.4 %collective-permute-start.26 = (bf16[640,640]{1,0:T(8,128)(2,1)}, bf16[640,640]{1,0:T(8,128)(2,1)}, u32[]{:S(2)}, u32[]{:S(2)}) collective-permute-start(bf16[640,640]{1,0:T(8,128)(2,1)} %bitcast.58), channel_id=1, source_target_pairs={{0,4},{2,6},{4,0},{6,2},{8,12},{10,14},{12,8},{14,10},{16,20},{18,... | collective-permute-start | bytes 2457608 | tf_op jit(solution)/shard_map/ppermute | solution.py:33
  169.9 30.2 %collective-permute-start.21 = (bf16[704,1280]{1,0:T(8,128)(2,1)}, bf16[704,1280]{1,0:T(8,128)(2,1)}, u32[]{:S(2)}, u32[]{:S(2)}) collective-permute-start(bf16[704,1280]{1,0:T(8,128)(2,1)} %convolution_convert_fusion.2), channel_id=1, source_target_pairs={{0,1},{1,0},{2,3},{3,2},{4,5},{5,4},{6,7},{7,6},{8,9},{9,8},{10,11... | collective-permute-start | bytes 5406728 | tf_op jit(solution)/shard_map/ppermute | solution.py:41
  211.3 28.4 %collective-permute-start.30 = (bf16[704,1280]{1,0:T(8,128)(2,1)}, bf16[704,1280]{1,0:T(8,128)(2,1)}, u32[]{:S(2)}, u32[]{:S(2)}) collective-permute-start(bf16[704,1280]{1,0:T(8,128)(2,1)} %convolution_convert_fusion), channel_id=1, source_target_pairs={{0,1},{1,0},{2,3},{3,2},{4,5},{5,4},{6,7},{7,6},{8,9},{9,8},{10,11... | collective-permute-start | bytes 5406728 | tf_op jit(solution)/shard_map/ppermute | solution.py:41
  334.5 73.3 %collective-permute-start.31 = (bf16[704,1280]{1,0:T(8,128)(2,1)}, bf16[704,1280]{1,0:T(8,128)(2,1)}, u32[]{:S(2)}, u32[]{:S(2)}) collective-permute-start(bf16[704,1280]{1,0:T(8,128)(2,1)} %fusion.13), channel_id=1, source_target_pairs={{0,1},{1,0},{2,3},{3,2},{4,5},{5,4},{6,7},{7,6},{8,9},{9,8},{10,11... | collective-permute-start | bytes 5406728 | tf_op jit(solution)/shard_map/ppermute | solution.py:41
  338.1 14.4 %collective-permute-start.46 = (bf16[320,640]{1,0:T(8,128)(2,1)}, bf16[320,640]{1,0:T(8,128)(2,1)}, u32[]{:S(2)}, u32[]{:S(2)}) collective-permute-start(bf16[320,640]{1,0:T(8,128)(2,1)} %bitcast.311), channel_id=1, source_target_pairs={{0,8},{2,10},{4,12},{6,14},{8,16},{10,18},{12,20},{14,22},{16,24},... | collective-permute-start | bytes 1228808 | tf_op jit(solution)/shard_map/ppermute | solution.py:37
  344.5 16.6 %collective-permute-start.39 = (bf16[320,640]{1,0:T(8,128)(2,1)S(1)}, bf16[320,640]{1,0:T(8,128)(2,1)S(1)}, u32[]{:S(2)}, u32[]{:S(2)}) collective-permute-start(bf16[320,640]{1,0:T(8,128)(2,1)S(1)} %bitcast.312), channel_id=1, source_target_pairs={{0,8},{2,10},{4,12},{6,14},{8,16},{10,18},{12,20},{14,22},{16,24},... | collective-permute-start | bytes 1228808 | tf_op jit(solution)/shard_map/ppermute | solution.py:37
  353.8 16.1 %collective-permute-start.47 = (bf16[320,640]{1,0:T(8,128)(2,1)S(1)}, bf16[320,640]{1,0:T(8,128)(2,1)S(1)}, u32[]{:S(2)}, u32[]{:S(2)}) collective-permute-start(bf16[320,640]{1,0:T(8,128)(2,1)S(1)} %fusion.32), channel_id=1, source_target_pairs={{0,8},{2,10},{4,12},{6,14},{8,16},{10,18},{12,20},{14,22},{16,24},... | collective-permute-start | bytes 1228808 | tf_op jit(solution)/shard_map/ppermute | solution.py:37
  362.0 19.2 %collective-permute-start.40 = (bf16[320,640]{1,0:T(8,128)(2,1)}, bf16[320,640]{1,0:T(8,128)(2,1)}, u32[]{:S(2)}, u32[]{:S(2)}) collective-permute-start(bf16[320,640]{1,0:T(8,128)(2,1)} %fusion.34), channel_id=1, source_target_pairs={{0,8},{2,10},{4,12},{6,14},{8,16},{10,18},{12,20},{14,22},{16,24},... | collective-permute-start | bytes 1228808 | tf_op jit(solution)/shard_map/ppermute | solution.py:37
  370.8 16.8 %collective-permute-start.48 = (bf16[320,640]{1,0:T(8,128)(2,1)}, bf16[320,640]{1,0:T(8,128)(2,1)}, u32[]{:S(2)}, u32[]{:S(2)}) collective-permute-start(bf16[320,640]{1,0:T(8,128)(2,1)} %fusion.33), channel_id=1, source_target_pairs={{0,8},{2,10},{4,12},{6,14},{8,16},{10,18},{12,20},{14,22},{16,24},... | collective-permute-start | bytes 1228808 | tf_op jit(solution)/shard_map/ppermute | solution.py:37
  436.6 20.0 %collective-permute-start.32 = (bf16[352,640]{1,0:T(8,128)(2,1)S(1)}, bf16[352,640]{1,0:T(8,128)(2,1)}, u32[]{:S(2)}, u32[]{:S(2)}) collective-permute-start(bf16[352,640]{1,0:T(8,128)(2,1)S(1)} %bitcast.304), channel_id=1, source_target_pairs={{0,4},{2,6},{4,0},{6,2},{8,12},{10,14},{12,8},{14,10},{16,20},{18,... | collective-permute-start | bytes 1351688 | tf_op jit(solution)/shard_map/ppermute | solution.py:33
  437.2 21.0 %collective-permute-start.34 = (bf16[352,640]{1,0:T(8,128)(2,1)S(1)}, bf16[352,640]{1,0:T(8,128)(2,1)}, u32[]{:S(2)}, u32[]{:S(2)}) collective-permute-start(bf16[352,640]{1,0:T(8,128)(2,1)S(1)} %bitcast.303), channel_id=1, source_target_pairs={{0,2},{2,0},{4,6},{6,4},{8,10},{10,8},{12,14},{14,12},{16,18},{18,... | collective-permute-start | bytes 1351688 | tf_op jit(solution)/shard_map/ppermute | solution.py:29
  449.9 27.4 %collective-permute-start.54 = (bf16[704,640]{1,0:T(8,128)(2,1)S(1)}, bf16[704,640]{1,0:T(8,128)(2,1)S(1)}, u32[]{:S(2)}, u32[]{:S(2)}) collective-permute-start(bf16[704,640]{1,0:T(8,128)(2,1)S(1)} %pad_maximum_fusion.12), channel_id=1, source_target_pairs={{0,2},{2,0},{4,6},{6,4},{8,10},{10,8},{12,14},{14,12},{16,18},{18,... | collective-permute-start | bytes 2703368 | tf_op jit(solution)/shard_map/ppermute | solution.py:29
  451.1 26.2 %collective-permute-start.56 = (bf16[704,640]{1,0:T(8,128)(2,1)S(1)}, bf16[704,640]{1,0:T(8,128)(2,1)S(1)}, u32[]{:S(2)}, u32[]{:S(2)}) collective-permute-start(bf16[704,640]{1,0:T(8,128)(2,1)S(1)} %pad_maximum_fusion.13), channel_id=1, source_target_pairs={{0,4},{2,6},{4,0},{6,2},{8,12},{10,14},{12,8},{14,10},{16,20},{18,... | collective-permute-start | bytes 2703368 | tf_op jit(solution)/shard_map/ppermute | solution.py:33
  459.7 33.1 %collective-permute-start.33 = (bf16[704,640]{1,0:T(8,128)(2,1)S(1)}, bf16[704,640]{1,0:T(8,128)(2,1)S(1)}, u32[]{:S(2)}, u32[]{:S(2)}) collective-permute-start(bf16[704,640]{1,0:T(8,128)(2,1)S(1)} %pad_maximum_fusion.10), channel_id=1, source_target_pairs={{0,2},{2,0},{4,6},{6,4},{8,10},{10,8},{12,14},{14,12},{16,18},{18,... | collective-permute-start | bytes 2703368 | tf_op jit(solution)/shard_map/ppermute | solution.py:29
  460.9 31.9 %collective-permute-start.35 = (bf16[704,640]{1,0:T(8,128)(2,1)S(1)}, bf16[704,640]{1,0:T(8,128)(2,1)S(1)}, u32[]{:S(2)}, u32[]{:S(2)}) collective-permute-start(bf16[704,640]{1,0:T(8,128)(2,1)S(1)} %pad_maximum_fusion.11), channel_id=1, source_target_pairs={{0,4},{2,6},{4,0},{6,2},{8,12},{10,14},{12,8},{14,10},{16,20},{18,... | collective-permute-start | bytes 2703368 | tf_op jit(solution)/shard_map/ppermute | solution.py:33
  477.7 15.5 %collective-permute-start.57 = (bf16[176,640]{1,0:T(8,128)(2,1)S(1)}, bf16[176,640]{1,0:T(8,128)(2,1)S(1)}, u32[]{:S(2)}, u32[]{:S(2)}) collective-permute-start(bf16[176,640]{1,0:T(8,128)(2,1)S(1)} %slice.617), channel_id=1, source_target_pairs={{0,8},{2,10},{4,12},{6,14},{8,16},{10,18},{12,20},{14,22},{16,24},... | collective-permute-start | bytes 675848 | tf_op jit(solution)/shard_map/ppermute | solution.py:37
  (106 other events, 758.4 us)

commit v2 on v1

v2 whole, which is shorter than its diff:
```python
import functools
import math

import jax
import jax.numpy as jnp
import numpy as np
from jax import lax
from jax.experimental import pallas as pl
from jax.experimental.pallas import tpu as pltpu
from jax.sharding import PartitionSpec as P

HD = 80
NCLASS = 3
PATCHES = 16
EXTRA = 16
TILE = 352
BLOCKS = {352: (128, 128, 96), 176: (96, 80)}[TILE]
LANES = 128
BF = jnp.bfloat16
F32 = jnp.float32
ROOT = math.sqrt(HD)
VMEM_LIMIT = 48 * 1024 * 1024


def pairs(move):
    out = []
    for z in range(4):
        for y in range(2):
            for x in range(2):
                a, b, c = move(z, y, x)
                out.append(((z * 2 + y) * 2 + x, (a * 2 + b) * 2 + c))
    return out


def over_x(field):
    return lax.ppermute(field, "dp", pairs(lambda z, y, x: (z, y, 1 - x)))


def over_y(field):
    return lax.ppermute(field, "dp", pairs(lambda z, y, x: (z, 1 - y, x)))


def up_z(field):
    return lax.ppermute(field, "dp", pairs(lambda z, y, x: ((z + 1) % 4, y, x)))


def up_z_two(field):
    return lax.ppermute(field, "dp", pairs(lambda z, y, x: ((z + 2) % 4, y, x)))


def over_mp(field):
    return lax.ppermute(field, "mp", [(0, 1), (1, 0)])


def gridded():
    return lax.axis_size("dp") == 16


def chip_order():
    me = lax.axis_index("dp")
    z, y, x = me // 4, (me // 2) % 2, me % 2
    k = jnp.arange(16, dtype=jnp.int32)
    line, square = k // 4, k % 4
    return ((z - line + 4) % 4) * 4 + (y ^ (square // 2)) * 2 + (x ^ (square % 2))


def gather_square_first(block):
    if not gridded():
        return ("whole", (lax.all_gather(block, "dp"),))
    half = block.shape[0] // 2
    from_x = over_x(block)
    from_y = over_y(block)
    first = over_y(from_x[:half])
    second = over_x(from_y[half:])
    parts = [jnp.concatenate([block, from_x, from_y, first, second]).reshape((4,) + block.shape)]
    for _ in range(3):
        parts.append(up_z(parts[-1]))
    return ("line", tuple(parts))


def gather_line_first(block):
    if not gridded():
        return ("whole", (lax.all_gather(block, "dp"),))
    parts = [block]
    for _ in range(3):
        parts.append(up_z(parts[-1]))
    own = jnp.stack(parts)
    from_x = over_x(own)
    from_y = over_y(own)
    first = over_y(from_x[:2])
    second = over_x(from_y[2:])
    return ("square", (own, from_x, from_y, first, second))


def pieces(kind):
    if kind == "line":
        return [(k, s, k, s) for k in range(4) for s in range(4)]
    out = [(s, k, k, s) for s in range(3) for k in range(4)]
    return out + [(3 + k // 2, k % 2, k, 3) for k in range(4)]


def scatter_square_sum(own, gx, gy, first, second):
    via_x = over_x(first)
    via_y = over_y(second)
    to_y = jnp.concatenate([(gy[:2].astype(F32) + via_x.astype(F32)).astype(BF), gy[2:]])
    to_x = jnp.concatenate([gx[:2], (gx[2:].astype(F32) + via_y.astype(F32)).astype(BF)])
    return own, over_x(to_x), over_y(to_y)


def scatter_square_first(parts):
    if not gridded():
        return lax.psum_scatter(parts[0].astype(F32), "dp", scatter_dimension=0, tiled=True)
    terms = scatter_square_sum(*parts)
    at = lambda k: sum(t[k].astype(F32) for t in terms)
    total = at(1)
    for k in (2, 3, 0):
        total = at(k) + up_z(total.astype(BF)).astype(F32)
    return total


def scatter_line_first(parts):
    if not gridded():
        return lax.psum_scatter(parts[0].astype(F32), "dp", scatter_dimension=0, tiled=True)
    total = parts[1]
    for k in (2, 3, 0):
        total = (parts[k].astype(F32) + up_z(total).astype(F32)).astype(BF)
    half = total.shape[1] // 2
    via_x = over_x(total[3, :half])
    via_y = over_y(total[3, half:])
    to_y = jnp.concatenate([(total[2, :half].astype(F32) + via_x.astype(F32)).astype(BF), total[2, half:]])
    to_x = jnp.concatenate([total[1, :half], (total[1, half:].astype(F32) + via_y.astype(F32)).astype(BF)])
    return total[0].astype(F32) + (over_x(to_x).astype(F32) + over_y(to_y).astype(F32))


def sum_small(field):
    if not gridded():
        return lax.psum(field, "dp")
    field = field + over_x(field)
    field = field + over_y(field)
    field = field + up_z_two(field)
    return field + lax.ppermute(field, "dp", pairs(lambda z, y, x: (z ^ 1, y, x)))


NN = (((1,), (0,)), ((), ()))
NT = (((1,), (1,)), ((), ()))
TN = (((0,), (0,)), ((), ()))


def dot(a, b, dims=NN):
    return lax.dot_general(a, b, dims, preferred_element_type=F32)


class Weights:
    def __init__(self, wanted, share):
        self.share = share
        self.wanted = wanted
        self.arrays = []
        for (kind, group), _, _ in wanted:
            for array in group:
                if not any(array is a for a in self.arrays):
                    self.arrays.append(array)

    def specs(self):
        return [pl.BlockSpec(memory_space=pl.ANY)] * len(self.arrays)

    def start(self, which, refs, order, into, sem):
        (kind, group), row, rows = self.wanted[which]
        find = lambda array: refs[[a is array for a in self.arrays].index(True)]
        if kind == "whole":
            chips = group[0].shape[0]
            if rows % 16 == 0 and row % 16 == 0:
                def body(c, carry):
                    to = into.at[pl.ds(pl.multiple_of(c * rows, 16), rows)]
                    pltpu.make_async_copy(find(group[0]).at[c, pl.ds(row, rows)], to, sem).start()
                    return carry
                lax.fori_loop(0, chips, body, 0)
            else:
                raise ValueError("rows")
            return
        for array, index, line, square in pieces(kind):
            chip = order[line * 4 + square]
            to = into.at[pl.ds(pl.multiple_of(chip * rows, 16), rows)]
            pltpu.make_async_copy(find(group[array]).at[index, pl.ds(row, rows)], to, sem).start()


def wait_all(into, sem):
    pltpu.make_async_copy(into, into, sem).wait()


def tile_spec(shape):
    if len(shape) == 3:
        return pl.BlockSpec((shape[0], TILE, shape[2]), lambda i: (0, i, 0))
    return pl.BlockSpec((TILE, shape[1]), lambda i: (i, 0))


def whole_spec(shape):
    return pl.BlockSpec(shape, lambda i: (0,) * len(shape))


def run(name, body, order, tiles, wholes, weights, out_tiles, out_wholes, scratch=(), flops=0, extra_bytes=0):
    tokens = tiles[0].shape[1] if tiles[0].ndim == 3 else tiles[0].shape[0]
    inputs = [order, *tiles, *wholes, *(weights.arrays if weights else ())]
    outs = [*out_tiles, *out_wholes]
    in_specs = [pl.BlockSpec(memory_space=pltpu.SMEM)]
    in_specs += [tile_spec(a.shape) for a in tiles] + [whole_spec(a.shape) for a in wholes]
    if weights:
        in_specs += weights.specs()
    cost = sum(math.prod(a.shape) * a.dtype.itemsize for a in [*inputs[1:], *outs])
    result = pl.pallas_call(
        body,
        name=name,
        grid=(tokens // TILE,),
        in_specs=in_specs,
        out_specs=[tile_spec(o.shape) for o in out_tiles] + [whole_spec(o.shape) for o in out_wholes],
        out_shape=outs,
        scratch_shapes=list(scratch),
        compiler_params=pltpu.CompilerParams(
            vmem_limit_bytes=VMEM_LIMIT, dimension_semantics=("arbitrary",)
        ),
        cost_estimate=pl.CostEstimate(flops=int(flops), bytes_accessed=int(cost), transcendentals=0),
    )(*inputs)
    return result


def window(h):
    first = h * HD // LANES
    return first, (h * HD + HD - 1) // LANES - first + 1


def head_lanes(h):
    first, count = window(h)
    lane = lax.broadcasted_iota(jnp.int32, (1, count * LANES), 1) + first * LANES
    return (lane >= h * HD) & (lane < h * HD + HD)


def columns(h):
    first, count = window(h)
    return slice(first * LANES, (first + count) * LANES)


def add_window(sums, h, part):
    first, count = window(h)
    for c in range(count):
        piece = part[:, c * LANES : (c + 1) * LANES]
        sums[first + c] = piece if sums[first + c] is None else sums[first + c] + piece


def rope(v, cos, left_sin, right_sin):
    rows, cols = v.shape
    left = pltpu.roll(v, cols - HD // 2, 1)
    right = pltpu.roll(v, HD // 2, 1)
    three = lambda f: f.reshape(rows // PATCHES, PATCHES, cols)
    out = three(v) * cos[...] + three(left) * left_sin + three(right) * right_sin
    return out.reshape(rows, cols)


def rope_tables(heads):
    half = HD // 2
    i = np.arange(half, dtype=np.float32)
    rates = np.exp(np.float32(-math.log(10000.0)) * (np.float32(2.0) * i / np.float32(HD))).astype(np.float32)
    angle = np.arange(PATCHES, dtype=np.float32)[:, None] * rates[None, :]
    cos, sin = np.cos(angle).astype(np.float32), np.sin(angle).astype(np.float32)
    zero = np.zeros_like(sin)
    full = lambda a, b: np.tile(np.concatenate([a, b], 1), (1, heads))
    return full(cos, cos), full(-sin, zero), full(zero, sin)


def row_of(small, at):
    return jnp.concatenate([small[at : at + 1, :], small[at + 1 : at + 2, :]], axis=1)


def token_weight(info, small):
    counts = [small[6:7, c : c + 1] * 16.0 + small[6:7, NCLASS + c : NCLASS + c + 1] for c in range(NCLASS)]
    total = counts[0] + counts[1] + counts[2]
    return sum(info[:, 1 + c : 2 + c] * (total / (NCLASS * counts[c])) for c in range(NCLASS))


def scale_of(field):
    return lax.rsqrt(jnp.mean(field * field, axis=-1, keepdims=True) + 1e-06)


def attention_forward(order, tokens, info, coderow, cos, left_sin, right_sin, weights, share, heads):
    cols, width = heads * HD, tokens.shape[1]
    chips = width // share
    count = tokens.shape[0]
    n_pieces = len(weights.arrays)

    def body(order, tokens, info, coderow, cos, left_sin, right_sin, *refs):
        got, refs = refs[:n_pieces], refs[n_pieces:]
        normed, q_out, k_out, v_out, probs, mixture, small, w, extras, sems = refs
        step = pl.program_id(0)

        @pl.when(step == 0)
        def _():
            weights.start(3, got, order, extras, sems.at[3])
            for n in range(3):
                weights.start(n, got, order, w.at[n], sems.at[n])
            wait_all(extras, sems.at[3])
            total = extras[pl.ds(0, EXTRA)].astype(F32)
            for c in range(1, chips):
                total = total + extras[pl.ds(c * EXTRA, EXTRA)].astype(F32)
            small[...] = total

        x = tokens[...].astype(F32)
        normed[...] = (x * scale_of(x) * row_of(small, 0)).astype(BF)

        @pl.when(step == 0)
        def _():
            for n in range(3):
                wait_all(w.at[n], sems.at[n])

        low = normed[...]
        q_out[...] = rope(dot(low, w[0]), cos, left_sin[...], right_sin[...]).astype(BF)
        k_out[...] = rope(dot(low, w[1]), cos, left_sin[...], right_sin[...]).astype(BF)
        v_out[...] = dot(low, w[2]).astype(BF)
        start = 0
        for b, size in enumerate(BLOCKS):
            rows = slice(start, start + size)
            key_at = lax.broadcasted_iota(jnp.int32, (size, size), 0)
            query_at = lax.broadcasted_iota(jnp.int32, (size, size), 1)
            same = info[rows, 0:1] == coderow[step * len(BLOCKS) + b][:, :size]
            allowed = (same & (key_at < query_at)) | (key_at == query_at)
            sums = [None] * (cols // LANES)
            for h in range(heads):
                here, lanes = columns(h), head_lanes(h)
                query = jnp.where(lanes, q_out[rows, here], jnp.zeros((), BF))
                scores = dot(k_out[rows, here], query, NT) * (1.0 / ROOT)
                scores = jnp.where(allowed, scores, -1e30)
                exponent = jnp.exp(scores - jnp.max(scores, axis=0, keepdims=True))
                soft = exponent * (1.0 / jnp.sum(exponent, axis=0, keepdims=True))
                probs[h, rows, 0:size] = soft
                value = jnp.where(lanes, v_out[rows, here], jnp.zeros((), BF))
                add_window(sums, h, dot(soft.astype(BF), value, TN))
            mixture[rows, :] = jnp.concatenate(sums, axis=1).astype(BF)
            start += size

    shape = jax.ShapeDtypeStruct
    return run(
        "attention_forward",
        body,
        order,
        [tokens, info],
        [coderow, cos, left_sin, right_sin],
        weights,
        [shape((count, width), BF)]
        + [shape((count, cols), BF)] * 3
        + [shape((heads, count, LANES), F32), shape((count, cols), BF)],
        [shape((EXTRA, cols), F32)],
        [
            pltpu.VMEM((3, width, cols), BF),
            pltpu.VMEM((chips * EXTRA, cols), BF),
            pltpu.SemaphoreType.DMA((4,)),
        ],
        flops=6 * count * width * cols,
    )


def attention_backward(order, q, k, v, probs, mixture_grad, cos, left_sin, right_sin, heads):
    count, cols = q.shape

    def body(order, q, k, v, probs, mg, cos, left_sin, right_sin, dq_out, dk_out, dv_out, dq, dk):
        start = 0
        zero = jnp.zeros((), BF)
        for size in BLOCKS:
            rows = slice(start, start + size)
            sums = [[None] * (cols // LANES) for _ in range(3)]
            for h in range(heads):
                here, lanes = columns(h), head_lanes(h)
                soft = probs[h, rows, 0:size]
                grad = jnp.where(lanes, mg[rows, here], zero)
                query = jnp.where(lanes, q[rows, here], zero)
                key = jnp.where(lanes, k[rows, here], zero)
                soft_grad = dot(v[rows, here], grad, NT)
                inner = jnp.sum(soft * soft_grad, axis=0, keepdims=True)
                score_grad = (soft * (soft_grad - inner)).astype(BF)
                add_window(sums[2], h, dot(soft.astype(BF), grad))
                add_window(sums[0], h, dot(score_grad, key, TN))
                add_window(sums[1], h, dot(score_grad, query))
            dv_out[rows, :] = jnp.concatenate(sums[2], axis=1).astype(BF)
            dq[rows, :] = jnp.concatenate(sums[0], axis=1)
            dk[rows, :] = jnp.concatenate(sums[1], axis=1)
            start += size
        for grad, out in ((dq, dq_out), (dk, dk_out)):
            turned = rope(grad[...] * (1.0 / ROOT), cos, -left_sin[...], -right_sin[...])
            out[...] = turned.astype(BF)

    shape = jax.ShapeDtypeStruct
    return run(
        "attention_backward",
        body,
        order,
        [q, k, v, probs, mixture_grad],
        [cos, left_sin, right_sin],
        None,
        [shape((count, cols), BF)] * 3,
        [],
        [pltpu.VMEM((TILE, cols), F32)] * 2,
        flops=12 * count * LANES * cols,
    )


def project_back(name, order, fields, weights):
    count, cols = fields[0].shape
    width = weights.share * (16 if weights.wanted[0][0][0] != "whole" else weights.wanted[0][0][1][0].shape[0])
    n_fields, n_pieces = len(fields), len(weights.arrays)

    def body(order, *refs):
        inputs, got = refs[:n_fields], refs[n_fields : n_fields + n_pieces]
        out, w, sems = refs[n_fields + n_pieces :]

        @pl.when(pl.program_id(0) == 0)
        def _():
            for n in range(n_fields):
                weights.start(n, got, order, w.at[n], sems.at[n])
            for n in range(n_fields):
                wait_all(w.at[n], sems.at[n])

        total = dot(inputs[0][...], w[0], NT)
        for n in range(1, n_fields):
            total = total + dot(inputs[n][...], w[n], NT)
        out[...] = total.astype(BF)

    return run(
        name,
        body,
        order,
        fields,
        [],
        weights,
        [jax.ShapeDtypeStruct((count, width), BF)],
        [],
        [pltpu.VMEM((n_fields, width, cols), BF), pltpu.SemaphoreType.DMA((n_fields,))],
        flops=2 * n_fields * count * width * cols,
    )[0]


def weigh_cotangent(order, cotangent, info, small):
    def body(order, cot, info, small, low, total):
        low[...] = (cot[...].astype(F32) * token_weight(info, small)).astype(BF)
        part = jnp.sum(low[...].astype(F32), axis=0, keepdims=True)
        total[...] = jnp.where(pl.program_id(0) == 0, part, total[...] + part)

    shape = jax.ShapeDtypeStruct
    return run(
        "weigh_cotangent",
        body,
        order,
        [cotangent, info],
        [small],
        None,
        [shape(cotangent.shape, BF)],
        [shape((1, cotangent.shape[1]), F32)],
    )


def mlp_up(order, tokens, mine, other, small, up_bias, weights):
    count, width = tokens.shape
    cols = up_bias.shape[1]
    n_pieces = len(weights.arrays)

    def body(order, tokens, mine, other, small, bias, *refs):
        got = refs[:n_pieces]
        hidden, normed, act, slope, w, sems = refs[n_pieces:]

        @pl.when(pl.program_id(0) == 0)
        def _():
            weights.start(0, got, order, w, sems.at[0])

        field = tokens[...].astype(F32) + (mine[...].astype(F32) + other[...].astype(F32))
        hidden[...] = field
        normed[...] = (field * scale_of(field) * row_of(small, 2)).astype(BF)

        @pl.when(pl.program_id(0) == 0)
        def _():
            wait_all(w, sems.at[0])

        pre = dot(normed[...], w[...]) + bias[...].astype(F32)
        sig = 1.0 / (1.0 + jnp.exp(-pre))
        act[...] = (pre * sig).astype(BF)
        slope[...] = sig * (1.0 + pre * (1.0 - sig))

    shape = jax.ShapeDtypeStruct
    return run(
        "mlp_up",
        body,
        order,
        [tokens, mine, other],
        [small, up_bias],
        weights,
        [shape((count, width), F32), shape((count, width), BF), shape((count, cols), BF), shape((count, cols), F32)],
        [],
        [pltpu.VMEM((width, cols), BF), pltpu.SemaphoreType.DMA((1,))],
        flops=2 * count * width * cols,
    )


def mlp_back(order, low, slope, weights):
    count, width = low.shape
    cols = slope.shape[1]
    n_pieces = len(weights.arrays)

    def body(order, low, slope, *refs):
        got = refs[:n_pieces]
        pre_grad, part, total, w, sems = refs[n_pieces:]

        @pl.when(pl.program_id(0) == 0)
        def _():
            for n in range(2):
                weights.start(n, got, order, w.at[n], sems.at[n])
            for n in range(2):
                wait_all(w.at[n], sems.at[n])

        pre_grad[...] = (dot(low[...], w[0]) * slope[...]).astype(BF)
        grad = pre_grad[...]
        here = jnp.sum(grad.astype(F32), axis=0, keepdims=True)
        total[...] = jnp.where(pl.program_id(0) == 0, here, total[...] + here)
        part[...] = dot(grad, w[1], NT).astype(BF)

    shape = jax.ShapeDtypeStruct
    return run(
        "mlp_back",
        body,
        order,
        [low, slope],
        [],
        weights,
        [shape((count, cols), BF), shape((count, width), BF)],
        [shape((1, cols), F32)],
        [pltpu.VMEM((2, width, cols), BF), pltpu.SemaphoreType.DMA((2,))],
        flops=4 * count * width * cols,
    )


def finish_output(order, hidden, mine, other, small):
    def body(order, hidden, mine, other, small, out):
        down = mine[...].astype(F32) + other[...].astype(F32)
        out[...] = (hidden[...] + (down + row_of(small, 4))).astype(BF)

    return run(
        "finish_output",
        body,
        order,
        [hidden, mine, other],
        [small],
        None,
        [jax.ShapeDtypeStruct(hidden.shape, BF)],
        [],
    )[0]


def hidden_back(order, hidden, mine, other, cotangent, info, small, weights):
    count, width = hidden.shape
    cols = small.shape[1]
    n_pieces = len(weights.arrays)

    def body(order, hidden, mine, other, cot, info, small, *refs):
        got = refs[:n_pieces]
        grad_out, low, mg, total, w, sems = refs[n_pieces:]

        @pl.when(pl.program_id(0) == 0)
        def _():
            weights.start(0, got, order, w, sems.at[0])

        field = hidden[...]
        scale = scale_of(field)
        grad = mine[...].astype(F32) + other[...].astype(F32)
        part = jnp.sum(grad * field * scale, axis=0, keepdims=True)
        total[...] = jnp.where(pl.program_id(0) == 0, part, total[...] + part)
        scaled = grad * row_of(small, 2)
        inner = jnp.mean(scaled * field, axis=-1, keepdims=True)
        upstream = cot[...].astype(F32) * token_weight(info, small)
        result = upstream + (scale * scaled - field * (scale * scale * scale * inner))
        grad_out[...] = result
        low[...] = result.astype(BF)

        @pl.when(pl.program_id(0) == 0)
        def _():
            wait_all(w, sems.at[0])

        mg[...] = dot(low[...], w[...]).astype(BF)

    shape = jax.ShapeDtypeStruct
    return run(
        "hidden_back",
        body,
        order,
        [hidden, mine, other, cotangent, info],
        [small],
        weights,
        [shape((count, width), F32), shape((count, width), BF), shape((count, cols), BF)],
        [shape((1, width), F32)],
        [pltpu.VMEM((width, cols), BF), pltpu.SemaphoreType.DMA((1,))],
        flops=2 * count * width * cols,
    )


def input_back(order, tokens, mine, other, hidden_grad, small):
    def body(order, tokens, mine, other, hidden_grad, small, out, total):
        field = tokens[...].astype(F32)
        scale = scale_of(field)
        grad = mine[...].astype(F32) + other[...].astype(F32)
        part = jnp.sum(grad * field * scale, axis=0, keepdims=True)
        total[...] = jnp.where(pl.program_id(0) == 0, part, total[...] + part)
        scaled = grad * row_of(small, 0)
        inner = jnp.mean(scaled * field, axis=-1, keepdims=True)
        out[...] = hidden_grad[...] + (scale * scaled - field * (scale * scale * scale * inner))

    shape = jax.ShapeDtypeStruct
    return run(
        "input_back",
        body,
        order,
        [tokens, mine, other, hidden_grad],
        [small],
        None,
        [shape(tokens.shape, F32)],
        [shape((1, tokens.shape[1]), F32)],
    )


def weight_grads(name, order, left, rights, kind, share):
    count, width = left.shape
    cols = rights[0].shape[1]
    step_cols = 256
    chips = width // share
    n = len(rights)
    rows = n * share
    if not gridded():
        outs = [(width * n, cols)]
    elif kind == "line":
        outs = [(4, rows, cols)] * 4
    else:
        outs = [(4, rows, cols)] * 3 + [(2, rows, cols)] * 2
    steps = width // step_cols
    meshed = gridded()

    def body(order, left, *refs):
        right, out, (scratch, sem) = refs[:n], refs[n:-2], refs[-2:]
        step = pl.program_id(0)
        for r in range(n):
            at = pl.ds(pl.multiple_of(step * step_cols, step_cols), step_cols)
            scratch[r, at, :] = dot(left[...], right[r][...], TN).astype(BF)

        @pl.when(step == steps - 1)
        def _():
            if not meshed:
                for r in range(n):
                    pltpu.make_async_copy(scratch.at[r], out[0].at[pl.ds(r * width, width)], sem).start()
            else:
                for array, index, line, square in pieces(kind):
                    chip = order[line * 4 + square]
                    for r in range(n):
                        pltpu.make_async_copy(
                            scratch.at[r, pl.ds(pl.multiple_of(chip * share, 16), share)],
                            out[array].at[index, pl.ds(r * share, share)],
                            sem,
                        ).start()
            wait_all(scratch, sem)

    result = pl.pallas_call(
        body,
        name=name,
        grid=(steps,),
        in_specs=[pl.BlockSpec(memory_space=pltpu.SMEM), pl.BlockSpec((count, step_cols), lambda i: (0, i))]
        + [whole_spec((count, cols))] * n,
        out_specs=[pl.BlockSpec(memory_space=pl.ANY)] * len(outs),
        out_shape=[jax.ShapeDtypeStruct(o, BF) for o in outs],
        scratch_shapes=[pltpu.VMEM((n, width, cols), BF), pltpu.SemaphoreType.DMA],
        compiler_params=pltpu.CompilerParams(
            vmem_limit_bytes=VMEM_LIMIT, dimension_semantics=("arbitrary",)
        ),
        cost_estimate=pl.CostEstimate(
            flops=2 * n * count * width * cols,
            bytes_accessed=2 * (count * width + n * count * cols + n * width * cols),
            transcendentals=0,
        ),
    )(order, left, *rights)
    if not meshed and n > 1:
        full = result[0].reshape(n, chips, share, cols)
        return [jnp.moveaxis(full, 0, 1).reshape(width * n, cols)]
    return result


def whole_blocks(gathered, row, rows):
    kind, (array,) = gathered
    part = array[:, row : row + rows]
    return ("whole", (part.reshape(1, -1, part.shape[2]),))


def local(
    tokens,
    cotangent,
    segment_ids,
    valid_mask,
    frequency,
    query_weight,
    key_weight,
    value_weight,
    output_weight,
    attn_gain,
    mlp_gain,
    up_weight,
    up_bias,
    down_weight,
    down_bias,
):
    dp = lax.axis_size("dp")
    me = lax.axis_index("dp")
    block_rows, patches = segment_ids.shape
    count, width = tokens.shape
    share, cols = query_weight.shape
    heads = cols // HD
    order = chip_order()

    member = (frequency == jnp.arange(NCLASS, dtype=jnp.int32)[None, :]).astype(jnp.int32)
    row_valid = jnp.sum(valid_mask, axis=1)
    local_counts = jnp.sum(member * row_valid[:, None], axis=0)
    here = (jnp.arange(dp, dtype=jnp.int32) == me)[:, None]
    vectors = jnp.stack([attn_gain, mlp_gain, down_bias])
    vectors = jnp.where(here[None], vectors[:, None, :], jnp.zeros((), BF)).reshape(6, cols)
    count_row = jnp.concatenate([local_counts // 16, local_counts % 16]).astype(BF)
    count_row = jnp.pad(count_row[None], ((0, 0), (0, cols - 2 * NCLASS)))
    extra = jnp.pad(jnp.concatenate([vectors, count_row]), ((0, EXTRA - 7), (0, 0)))

    code = (jnp.arange(block_rows, dtype=jnp.int32)[:, None] * PATCHES + segment_ids).astype(F32)
    of_class = (valid_mask[:, :, None] * member[:, None, :]).astype(F32).reshape(count, NCLASS)
    key_code = jnp.where(valid_mask == 1, code, -1.0).reshape(count, 1)
    info = jnp.pad(jnp.concatenate([key_code, of_class], 1), ((0, 0), (0, 7 - NCLASS)))
    flat, rows, start = code.reshape(1, count), [], 0
    for _ in range(count // TILE):
        for size in BLOCKS:
            rows.append(jnp.pad(flat[:, start : start + size], ((0, 0), (0, LANES - size))))
            start += size
    coderow = jnp.stack(rows)
    tables = rope_tables(heads)

    got_qk = gather_line_first(jnp.concatenate([query_weight, key_weight, extra]))
    got_v = gather_square_first(value_weight)
    output_rows, down_rows = output_weight.T, down_weight.T
    got_qk_own, output_rows, up_rows, down_rows = lax.optimization_barrier(
        (got_qk[1][0], output_rows, up_weight, down_rows)
    )
    got_qk = (got_qk[0], (got_qk_own,) + got_qk[1][1:])
    got_o = gather_line_first(output_rows)
    got_ud = gather_line_first(jnp.concatenate([up_rows, down_rows]))
    if gridded():
        parts = {
            "q": (got_qk, 0, share),
            "k": (got_qk, share, share),
            "e": (got_qk, 2 * share, EXTRA),
            "v": (got_v, 0, share),
            "o": (got_o, 0, share),
            "u": (got_ud, 0, share),
            "d": (got_ud, share, share),
        }
    else:
        parts = {
            "q": (whole_blocks(got_qk, 0, share), 0, width),
            "k": (whole_blocks(got_qk, share, share), 0, width),
            "e": (whole_blocks(got_qk, 2 * share, EXTRA), 0, dp * EXTRA),
            "v": (whole_blocks(got_v, 0, share), 0, width),
            "o": (whole_blocks(got_o, 0, share), 0, width),
            "u": (whole_blocks(got_ud, 0, share), 0, width),
            "d": (whole_blocks(got_ud, share, share), 0, width),
        }
    take = lambda names: Weights([parts[n] for n in names], width // 16 if gridded() else width)

    normed_one, queries, keys, values, probs, mixture, small = attention_forward(
        order, tokens, info, coderow, *tables, take("qkve"), share, heads
    )
    attn_part = project_back("attention_out", order, [mixture], take("o"))
    attn_other = over_mp(attn_part)
    down_low, down_bias_sum = weigh_cotangent(order, cotangent, info, small)
    hidden, normed_two, activated, slope = mlp_up(
        order, tokens, attn_part, attn_other, small, up_bias[None], take("u")
    )
    pre_grad, normed_two_part, up_bias_sum = mlp_back(order, down_low, slope, take("du"))
    normed_two_other = over_mp(normed_two_part)
    down_part = project_back("mlp_down", order, [activated], take("d"))
    down_other = over_mp(down_part)
    up_local = weight_grads("up_grads", order, normed_two, [pre_grad], "square", share)
    down_local = weight_grads("down_grads", order, down_low, [activated], "square", share)
    layer_out = finish_output(order, hidden, down_part, down_other, small)
    hidden_grad, attn_low, mixture_grad, mlp_gain_sum = hidden_back(
        order, hidden, normed_two_part, normed_two_other, cotangent, info, small, take("o")
    )
    output_local = weight_grads("output_grads", order, attn_low, [mixture], "square", share)
    query_pre_grad, key_pre_grad, value_pre_grad = attention_backward(
        order, queries, keys, values, probs, mixture_grad, *tables, heads
    )
    value_local = weight_grads("value_grads", order, normed_one, [value_pre_grad], "line", share)
    qk_local = weight_grads(
        "query_key_grads", order, normed_one, [query_pre_grad, key_pre_grad], "square", share
    )
    normed_one_part = project_back(
        "attention_in_back", order, [query_pre_grad, key_pre_grad, value_pre_grad], take("qkv")
    )
    normed_one_other = over_mp(normed_one_part)
    input_grad, attn_gain_sum = input_back(
        order, tokens, normed_one_part, normed_one_other, hidden_grad, small
    )

    down_grad = scatter_square_first(down_local)
    up_grad = scatter_square_first(up_local)
    output_grad = scatter_square_first(output_local)
    value_grad = scatter_line_first(value_local)
    qk_grad = scatter_square_first(qk_local)
    sums = sum_small(
        jnp.concatenate(
            [s.reshape(-1, cols) for s in (attn_gain_sum, mlp_gain_sum, down_bias_sum, up_bias_sum)]
            + [jnp.zeros((1, cols), F32)]
        )
    )
    own = lax.dynamic_slice_in_dim(sums[:6].reshape(3, dp, share), me, 1, 1)[:, 0]
    return (
        layer_out,
        input_grad,
        qk_grad[:share],
        qk_grad[share:],
        value_grad,
        output_grad.T,
        own[0],
        own[1],
        up_grad,
        sums[6],
        down_grad.T,
        own[2],
    )


def solution(mesh):
    rows = P("dp", None)
    wide = P("dp", "mp")
    tall = P("mp", "dp")
    return jax.shard_map(
        local,
        mesh=mesh,
        in_specs=(rows,) * 5
        + (wide, wide, wide, tall, P("dp"), P("dp"), wide, P("mp"), tall, P("dp")),
        out_specs=(rows, rows, wide, wide, wide, tall, P("dp"), P("dp"), wide, P("mp"), tall, P("dp")),
        check_vma=False,
    )
```

time: 530 us -> 411 us (0.78); the launches traced: 521 us -> 409 us
  Pallas kernels: 0 us -> 124 us
  local copies, waits for them, and re-layouts: 136 us -> 30.5 us
  other arithmetic: 112 us -> 35.3 us
  matrix products: 75.6 us -> 0 us
  waiting for transfers between devices: 146 us -> 169 us
    pallas_call x0 -> x16, Pallas kernels: none -> 124 us  [the longest x11 92.4 us: run(): pl.pallas_call(body, name=name, grid=(tokens // TILE,), in_specs=in_specs...]
    dot_general x24 -> x0, matrix products: 75.6 us -> none  [the longest x1 5.59 us: local(): key_pre = jnp.dot(normed_one, wk_full, preferred_element_type=jnp.float32)]
    gather x8 -> x0, local copies, waits for them, and re-layouts: 38.6 us -> none  [the longest x2 14.3 us: scatter_rows(): two = jnp.take(second, (sa[:, None] + za[None, :] * 4).reshape(-1), axis=0)]
    convert_element_type x13 -> x1, local copies, waits for them, and re-layouts: 38.4 us -> 0.09 us  [local(): (jnp.arange(block_rows, dtype=jnp.int32)[:, None] * PATCHES + segment_ids...]
    another operation x26 -> x5, other arithmetic: 33.5 us -> 3.06 us  [the longest x4 2.36 us: gather_line_first(): own = jnp.stack(parts)]
    ppermute x24 -> x27, waiting for transfers between devices: 87.6 us -> 113 us  [up_z(): return lax.ppermute(field, 'dp', pairs(lambda z, y, x: ((z + 1) % 4, y, x)))]
    ppermute x16 -> x19, waiting for transfers between devices: 35.5 us -> 12 us  [over_x(): return lax.ppermute(field, 'dp', pairs(lambda z, y, x: (z, y, 1 - x)))]
    ppermute x16 -> x19, waiting for transfers between devices: 22.4 us -> 41.5 us  [over_y(): return lax.ppermute(field, 'dp', pairs(lambda z, y, x: (z, 1 - y, x)))]
  transfers between devices with their start and end apart: 60 -> 71, of which waited for: 31 -> 36; matrix products, arithmetic and copies ran while one was open for 34% -> 11% of each run, Pallas kernels for 0% -> 27%
where the time goes in v2:
time: 411 us; the launch traced here: 409 us
  waiting for transfers between devices  169 us (41%)
  Pallas kernels  124 us (30%)
  starting transfers between devices  48.4 us (12%)
  other arithmetic  35.3 us (9%)
  local copies, waits for them, and re-layouts  30.5 us (7%)
    ppermute x27, waiting for transfers between devices, up_z(): return lax.ppermute(field, 'dp', pairs(lambda z, y, x: ((z + 1) % 4, y, x)))  113 us
    pallas_call x11, Pallas kernels, run(): pl.pallas_call(body, name=name, grid=(tokens // TILE,), in_specs=in_specs...  92.4 us
    ppermute x19, waiting for transfers between devices, over_y(): return lax.ppermute(field, 'dp', pairs(lambda z, y, x: (z, 1 - y, x)))  41.5 us
    pallas_call x5, Pallas kernels, weight_grads(): pl.pallas_call(body, name=name, grid=(steps,), in_specs=[pl.BlockSpec(mem...  31.7 us
    unnamed x177, local copies, waits for them, and re-layouts  23.7 us
    ppermute x19, starting transfers between devices, over_x(): return lax.ppermute(field, 'dp', pairs(lambda z, y, x: (z, y, 1 - x)))  22.3 us
    ppermute x19, starting transfers between devices, over_y(): return lax.ppermute(field, 'dp', pairs(lambda z, y, x: (z, 1 - y, x)))  17.8 us
    ppermute x19, waiting for transfers between devices, over_x(): return lax.ppermute(field, 'dp', pairs(lambda z, y, x: (z, y, 1 - x)))  12 us
  transfers between devices with their start and end apart: 71, of which 36 were waited for; matrix products, arithmetic and copies ran while one was open for 11% of the time, Pallas kernels for 27%

profile of v2, /device:TPU:0, one launch (start us, length us, event | category | flops | bytes accessed | tf_op | source)
XLA Modules:
  0.0 409.4 jit_solution(12788149537696419786)
XLA Ops:
  17.3 7.7 %collective-permute-done.1 = bf16[176,640]{1,0:T(8,128)(2,1)S(1)} collective-permute-done((bf16[176,640]{1,0:T(8,128)(2,1)S(1)}, bf16[176,640]{1,0:T(8,128)(2,1)S(1)}, u32[]{:S(2)}, u32[]{:S(2)}) %collective-permute-start.1) | collective-permute-done | bytes 225312 | tf_op jit(solution)/shard_map/ppermute | solution.py:44
  25.5 9.8 %collective-permute-done.2 = bf16[176,640]{1,0:T(8,128)(2,1)S(1)} collective-permute-done((bf16[176,640]{1,0:T(8,128)(2,1)S(1)}, bf16[176,640]{1,0:T(8,128)(2,1)S(1)}, u32[]{:S(2)}, u32[]{:S(2)}) %collective-permute-start.2) | collective-permute-done | bytes 225312 | tf_op jit(solution)/shard_map/ppermute | solution.py:44
  40.4 11.7 %collective-permute-done.14 = bf16[80,640]{1,0:T(8,128)(2,1)} collective-permute-done((bf16[80,640]{1,0:T(8,128)(2,1)}, bf16[80,640]{1,0:T(8,128)(2,1)}, u32[]{:S(2)}, u32[]{:S(2)}) %collective-permute-start.14) | collective-permute-done | bytes 102432 | tf_op jit(solution)/shard_map/ppermute | solution.py:44
  52.4 7.6 %collective-permute-done.15 = bf16[80,640]{1,0:T(8,128)(2,1)} collective-permute-done((bf16[80,640]{1,0:T(8,128)(2,1)}, bf16[80,640]{1,0:T(8,128)(2,1)}, u32[]{:S(2)}, u32[]{:S(2)}) %collective-permute-start.15) | collective-permute-done | bytes 102432 | tf_op jit(solution)/shard_map/ppermute | solution.py:44
  60.3 6.4 %collective-permute-done.16 = bf16[80,640]{1,0:T(8,128)(2,1)} collective-permute-done((bf16[80,640]{1,0:T(8,128)(2,1)}, bf16[80,640]{1,0:T(8,128)(2,1)}, u32[]{:S(2)}, u32[]{:S(2)}) %collective-permute-start.16) | collective-permute-done | bytes 102432 | tf_op jit(solution)/shard_map/ppermute | solution.py:44
  84.7 20.0 %attention_forward.1 = (bf16[704,1280]{1,0:T(8,128)(2,1)}, bf16[704,640]{1,0:T(8,128)(2,1)S(1)}, bf16[704,640]{1,0:T(8,128)(2,1)S(1)}, bf16[704,640]{1,0:T(8,128...) custom-call(s32[16]{0:T(128)S(1)} %fusion.28.order, ...), custom_call_target="tpu_custom_call" | custom-call | flops 3460300800 | bytes 15524864 | tf_op jit(solution)/shard_map/attention_forward/pallas_call | solution.py:209
  111.6 9.2 %collective-permute-done.23 = bf16[160,640]{1,0:T(8,128)(2,1)S(1)} collective-permute-done((bf16[160,640]{1,0:T(8,128)(2,1)S(1)}, bf16[160,640]{1,0:T(8,128)(2,1)S(1)}, u32[]{:S(2)}, u32[]{:S(2)}) %collective-permute-start.23) | collective-permute-done | bytes 204832 | tf_op jit(solution)/shard_map/ppermute | solution.py:44
  120.8 8.4 %collective-permute-done.24 = bf16[160,640]{1,0:T(8,128)(2,1)S(1)} collective-permute-done((bf16[160,640]{1,0:T(8,128)(2,1)S(1)}, bf16[160,640]{1,0:T(8,128)(2,1)S(1)}, u32[]{:S(2)}, u32[]{:S(2)}) %collective-permute-start.24) | collective-permute-done | bytes 204832 | tf_op jit(solution)/shard_map/ppermute | solution.py:44
  131.4 16.8 %collective-permute-done.26.refs_2_.refs_3_ = bf16[4,160,640]{2,1,0:T(8,128)(2,1)S(1)} collective-permute-done((bf16[4,160,640]{2,1,0:T(8,128)(2,1)S(1)}, bf16[4,160,640]{2,1,0:T(8,128)(2,1)S(1)}, u32[]{:S(2)}, u32[]{:S(2)}) %collective-permute-start.26) | collective-permute-done | bytes 819232 | tf_op jit(solution)/shard_map/ppermute | solution.py:40
  152.5 5.8 %collective-permute-done.28.refs_4_.refs_5_ = bf16[2,160,640]{2,1,0:T(8,128)(2,1)S(1)} collective-permute-done((bf16[2,160,640]{2,1,0:T(8,128)(2,1)S(1)}, bf16[2,160,640]{2,1,0:T(8,128)(2,1)S(1)}, u32[]{:S(2)}, u32[]{:S(2)}) %collective-permute-start.28) | collective-permute-done | bytes 409632 | tf_op jit(solution)/shard_map/ppermute | solution.py:36
  160.0 8.8 %mlp_up.1 = (f32[704,1280]{1,0:T(8,128)}, bf16[704,1280]{1,0:T(8,128)(2,1)S(1)}, bf16[704,640]{1,0:T(8,128)(2,1)S(1)}, f32[704,640]{1,0:T(8,128)}) custom-call(s32[16]{0:T(128)S(1)} %fusion.28.order, bf16[704,1280]{1,0:T(8,128)(2,1)} %tokens.5, bf16[704,1280]{1,0:T(8,128)(2,1)} %copy-done.1, bf16[704,1280]{1,0:T(8,128)(2,1)} %copy-done.76, ...), custom_call_target="tpu_custom_call" | custom-call | flops 1153433600 | bytes 16835840 | tf_op jit(solution)/shard_map/mlp_up/pallas_call | solution.py:209
  175.2 10.5 %mlp_back.1 = (bf16[704,640]{1,0:T(8,128)(2,1)S(1)}, bf16[704,1280]{1,0:T(8,128)(2,1)}, f32[1,640]{1,0:T(1,128)S(1)}) custom-call(s32[16]{0:T(128)S(1)} %fusion.28.order, bf16[704,1280]{1,0:T(8,128)(2,1)} %copy-done.50, f32[704,640]{1,0:T(8,128)} %get-tuple-element.78.slope, bf16[4,160,640]{2,1,0:T(8,128)(2,1)S(1)} %pad_maximum_fusion.1.refs_0_.refs_1_, ...), custom_call_target="tpu_custom_call" | custom-call | flops 2306867200 | bytes 9587200 | tf_op jit(solution)/shard_map/mlp_back/pallas_call | solution.py:209
  196.3 7.5 %collective-permute-done.64 = bf16[2,80,640]{2,1,0:T(8,128)(2,1)S(1)} collective-permute-done((bf16[2,80,640]{2,1,0:T(8,128)(2,1)S(1)}, bf16[2,80,640]{2,1,0:T(8,128)(2,1)S(1)}, u32[]{:S(2)}, u32[]{:S(2)}) %collective-permute-start.64) | collective-permute-done | bytes 204832 | tf_op jit(solution)/shard_map/ppermute | solution.py:40
  221.8 6.4 %collective-permute-done.68 = bf16[80,640]{1,0:T(8,128)(2,1)S(1)} collective-permute-done((bf16[80,640]{1,0:T(8,128)(2,1)S(1)}, bf16[80,640]{1,0:T(8,128)(2,1)S(1)}, u32[]{:S(2)}, u32[]{:S(2)}) %collective-permute-start.68) | collective-permute-done | bytes 102432 | tf_op jit(solution)/shard_map/ppermute | solution.py:44
  230.7 5.9 %collective-permute-done.69 = bf16[80,640]{1,0:T(8,128)(2,1)S(1)} collective-permute-done((bf16[80,640]{1,0:T(8,128)(2,1)S(1)}, bf16[80,640]{1,0:T(8,128)(2,1)S(1)}, u32[]{:S(2)}, u32[]{:S(2)}) %collective-permute-start.69) | collective-permute-done | bytes 102432 | tf_op jit(solution)/shard_map/ppermute | solution.py:44
  246.6 9.9 %hidden_back.1 = (f32[704,1280]{1,0:T(8,128)}, bf16[704,1280]{1,0:T(8,128)(2,1)S(1)}, bf16[704,640]{1,0:T(8,128)(2,1)S(1)}, f32[1,1280]{1,0:T(1,128)S(1)}) custom-call(s32[16]{0:T(128)S(1)} %fusion.28.order, f32[704,1280]{1,0:T(8,128)} %get-tuple-element.71.hidden, bf16[704,1280]{1,0:T(8,128)(2,1)} %get-tuple-element.79.mine, ...), custom_call_target="tpu_custom_call" | custom-call | flops 1153433600 | bytes 17026048 | tf_op jit(solution)/shard_map/hidden_back/pallas_call | solution.py:209
  260.2 5.7 %output_grads.1 = (bf16[4,80,640]{2,1,0:T(8,128)(2,1)S(1)}, bf16[4,80,640]{2,1,0:T(8,128)(2,1)S(1)}, bf16[4,80,640]{2,1,0:T(8,128)(2,1)S(1)}, bf16[2,80,640]{2,1,0:T(8,128)(2,1)}, bf16[2,80,640]{2,1,0:T(8,128)(2,1)}) custom-call(s32[16]{0:T(128)S(1)} %fusion.28.order, bf16[704,1280]{1,0:T(8,128)(2,1)S(1)} %copy-done.52, bf16[704,640]{1,0:T(8,128)(2,1)S(1)} %copy-done.20), custom_call_target="tpu_custom_call" | custom-call | flops 1153433600 | bytes 4341760 | tf_op jit(solution)/shard_map/output_grads/pallas_call | solution.py:660
  269.3 12.5 %attention_backward.1 = (bf16[704,640]{1,0:T(8,128)(2,1)S(1)}, bf16[704,640]{1,0:T(8,128)(2,1)S(1)}, bf16[704,640]{1,0:T(8,128)(2,1)S(1)}) custom-call(s32[16]{0:T(128)S(1)} %fusion.28.order, bf16[704,640]{1,0:T(8,128)(2,1)S(1)} %copy-done.26, bf16[704,640]{1,0:T(8,128)(2,1)S(1)} %copy-done.28, bf16[704,640]{1,0:T(8,128)(2,1)S(1)} %copy-done.30, ...), custom_call_target="tpu_custom_call" | custom-call | flops 692060160 | bytes 9314304 | tf_op jit(solution)/shard_map/attention_backward/pallas_call | solution.py:209
  289.3 9.9 %query_key_grads.1 = (bf16[4,160,640]{2,1,0:T(8,128)(2,1)S(1)}, bf16[4,160,640]{2,1,0:T(8,128)(2,1)S(1)}, bf16[4,160,640]{2,1,0:T(8,128)(2,1)S(1)}, bf16[2,160,6...) custom-call(s32[16]{0:T(128)S(1)} %fusion.28.order, bf16[704,1280]{1,0:T(8,128)(2,1)} %get-tuple-element.86.left, ...), custom_call_target="tpu_custom_call" | custom-call | flops 2306867200 | bytes 6881280 | tf_op jit(solution)/shard_map/query_key_grads/pallas_call | solution.py:660
  304.5 10.8 %attention_in_back.1.mine = bf16[704,1280]{1,0:T(8,128)(2,1)} custom-call(s32[16]{0:T(128)S(1)} %fusion.28.order, bf16[704,640]{1,0:T(8,128)(2,1)S(1)} %copy-done.55, bf16[704,640]{1,0:T(8,128)(2,1)S(1)} %copy-done.58, bf16[704,640]{1,0:T(8,128)(2,1)S(1)} %copy-done.60, bf16[4,176,640]{2,1,0:T(8,128)(2,1)S(1)} %copy-done.24, ...), custom_call_target="tpu_custom_call" | custom-call | flops 3460300800 | bytes 9748480 | tf_op jit(solution)/shard_map/attention_in_back/pallas_call | solution.py:209
  320.8 6.9 %collective-permute-done.32 = bf16[2,160,640]{2,1,0:T(8,128)(2,1)S(1)} collective-permute-done((bf16[2,160,640]{2,1,0:T(8,128)(2,1)S(1)}, bf16[2,160,640]{2,1,0:T(8,128)(2,1)S(1)}, u32[]{:S(2)}, u32[]{:S(2)}) %collective-permute-start.32) | collective-permute-done | bytes 409632 | tf_op jit(solution)/shard_map/ppermute | solution.py:40
  338.3 10.6 %collective-permute-done.50 = bf16[80,640]{1,0:T(8,128)(2,1)S(1)} collective-permute-done((bf16[80,640]{1,0:T(8,128)(2,1)S(1)}, bf16[80,640]{1,0:T(8,128)(2,1)S(1)}, u32[]{:S(2)}, u32[]{:S(2)}) %collective-permute-start.50) | collective-permute-done | bytes 102432 | tf_op jit(solution)/shard_map/ppermute | solution.py:44
  349.6 6.3 %collective-permute-done.51 = bf16[80,640]{1,0:T(8,128)(2,1)S(1)} collective-permute-done((bf16[80,640]{1,0:T(8,128)(2,1)S(1)}, bf16[80,640]{1,0:T(8,128)(2,1)S(1)}, u32[]{:S(2)}, u32[]{:S(2)}) %collective-permute-start.51) | collective-permute-done | bytes 102432 | tf_op jit(solution)/shard_map/ppermute | solution.py:44
  375.3 8.1 %collective-permute-done.36 = bf16[160,640]{1,0:T(8,128)(2,1)S(1)} collective-permute-done((bf16[160,640]{1,0:T(8,128)(2,1)S(1)}, bf16[160,640]{1,0:T(8,128)(2,1)S(1)}, u32[]{:S(2)}, u32[]{:S(2)}) %collective-permute-start.36) | collective-permute-done | bytes 204832 | tf_op jit(solution)/shard_map/ppermute | solution.py:44
  (416 shorter events, 184.1 us)
Async XLA Ops:
  25.1 15.2 %collective-permute-start.11 = (bf16[4,80,640]{2,1,0:T(8,128)(2,1)S(1)}, bf16[4,80,640]{2,1,0:T(8,128)(2,1)S(1)}, u32[]{:S(2)}, u32[]{:S(2)}) collective-permute-start(bf16[4,80,640]{2,1,0:T(8,128)(2,1)S(1)} %bitcast.132), channel_id=1, source_target_pairs={{0,8},{2,10},{4,12},{6,14},{8,16},{10,18},{12,20},{14,22},{16,24},... | collective-permute-start | bytes 1228808 | tf_op jit(solution)/shard_map/ppermute | solution.py:44
  35.4 34.2 %collective-permute-start.4 = (bf16[4,176,640]{2,1,0:T(8,128)(2,1)S(1)}, bf16[4,176,640]{2,1,0:T(8,128)(2,1)S(1)}, u32[]{:S(2)}, u32[]{:S(2)}) collective-permute-start(bf16[4,176,640]{2,1,0:T(8,128)(2,1)S(1)} %pad_maximum_fusion.refs_0_.refs_3_), channel_id=1, source_target_pairs={{0,4},{2,6},{4,0},{6,2},{8,12},{10,14},{12,8},{14,10},{16,20},{18,... | collective-permute-start | bytes 2703368 | tf_op jit(solution)/shard_map/ppermute | solution.py:40
  36.0 34.6 %collective-permute-start.3 = (bf16[4,176,640]{2,1,0:T(8,128)(2,1)S(1)}, bf16[4,176,640]{2,1,0:T(8,128)(2,1)}, u32[]{:S(2)}, u32[]{:S(2)}) collective-permute-start(bf16[4,176,640]{2,1,0:T(8,128)(2,1)S(1)} %pad_maximum_fusion.refs_0_.refs_3_), channel_id=1, source_target_pairs={{0,2},{2,0},{4,6},{6,4},{8,10},{10,8},{12,14},{14,12},{16,18},{18,... | collective-permute-start | bytes 2703368 | tf_op jit(solution)/shard_map/ppermute | solution.py:36
  40.3 19.9 %collective-permute-start.12 = (bf16[4,80,640]{2,1,0:T(8,128)(2,1)S(1)}, bf16[4,80,640]{2,1,0:T(8,128)(2,1)S(1)}, u32[]{:S(2)}, u32[]{:S(2)}) collective-permute-start(bf16[4,80,640]{2,1,0:T(8,128)(2,1)S(1)} %collective-permute-done.11.refs_6_.refs_9_), channel_id=1, source_target_pairs={{0,8},{2,10},{4,12},{6,14},{8,16},{10,18},{12,20},{14,22},{16,24},... | collective-permute-start | bytes 1228808 | tf_op jit(solution)/shard_map/ppermute | solution.py:44
  60.3 20.9 %collective-permute-start.13 = (bf16[4,80,640]{2,1,0:T(8,128)(2,1)S(1)}, bf16[4,80,640]{2,1,0:T(8,128)(2,1)S(1)}, u32[]{:S(2)}, u32[]{:S(2)}) collective-permute-start(bf16[4,80,640]{2,1,0:T(8,128)(2,1)S(1)} %collective-permute-done.12.refs_7_.refs_10_), channel_id=1, source_target_pairs={{0,8},{2,10},{4,12},{6,14},{8,16},{10,18},{12,20},{14,22},{16,24},... | collective-permute-start | bytes 1228808 | tf_op jit(solution)/shard_map/ppermute | solution.py:44
  79.6 31.9 %collective-permute-start.22 = (bf16[160,640]{1,0:T(8,128)(2,1)S(1)}, bf16[160,640]{1,0:T(8,128)(2,1)S(1)}, u32[]{:S(2)}, u32[]{:S(2)}) collective-permute-start(bf16[160,640]{1,0:T(8,128)(2,1)S(1)} %constant_dynamic-update-slice_fusion.11), channel_id=1, source_target_pairs={{0,8},{2,10},{4,12},{6,14},{8,16},{10,18},{12,20},{14,22},{16,24},... | collective-permute-start | bytes 614408 | tf_op jit(solution)/shard_map/ppermute | solution.py:44
  79.8 24.9 %collective-permute-start.20 = (bf16[2,80,640]{2,1,0:T(8,128)(2,1)S(1)}, bf16[2,80,640]{2,1,0:T(8,128)(2,1)S(1)}, u32[]{:S(2)}, u32[]{:S(2)}) collective-permute-start(bf16[2,80,640]{2,1,0:T(8,128)(2,1)S(1)} %slice.382), channel_id=1, source_target_pairs={{0,2},{2,0},{4,6},{6,4},{8,10},{10,8},{12,14},{14,12},{16,18},{18,... | collective-permute-start | bytes 614408 | tf_op jit(solution)/shard_map/ppermute | solution.py:36
  81.2 23.6 %collective-permute-start.19 = (bf16[2,80,640]{2,1,0:T(8,128)(2,1)S(1)}, bf16[2,80,640]{2,1,0:T(8,128)(2,1)S(1)}, u32[]{:S(2)}, u32[]{:S(2)}) collective-permute-start(bf16[2,80,640]{2,1,0:T(8,128)(2,1)S(1)} %slice.381), channel_id=1, source_target_pairs={{0,4},{2,6},{4,0},{6,2},{8,12},{10,14},{12,8},{14,10},{16,20},{18,... | collective-permute-start | bytes 614408 | tf_op jit(solution)/shard_map/ppermute | solution.py:40
  111.4 47.3 %collective-permute-start.21 = (bf16[704,1280]{1,0:T(8,128)(2,1)S(1)}, bf16[704,1280]{1,0:T(8,128)(2,1)S(1)}, u32[]{:S(2)}, u32[]{:S(2)}) collective-permute-start(bf16[704,1280]{1,0:T(8,128)(2,1)S(1)} %attention_out.1.mine), channel_id=1, source_target_pairs={{0,1},{1,0},{2,3},{3,2},{4,5},{5,4},{6,7},{7,6},{8,9},{9,8},{10,11... | collective-permute-start | bytes 5406728 | tf_op jit(solution)/shard_map/ppermute | solution.py:52
  129.3 19.0 %collective-permute-start.26 = (bf16[4,160,640]{2,1,0:T(8,128)(2,1)S(1)}, bf16[4,160,640]{2,1,0:T(8,128)(2,1)S(1)}, u32[]{:S(2)}, u32[]{:S(2)}) collective-permute-start(bf16[4,160,640]{2,1,0:T(8,128)(2,1)S(1)} %pad_maximum_fusion.1.refs_0_.refs_1_), channel_id=1, source_target_pairs={{0,4},{2,6},{4,0},{6,2},{8,12},{10,14},{12,8},{14,10},{16,20},{18,... | collective-permute-start | bytes 2457608 | tf_op jit(solution)/shard_map/ppermute | solution.py:40
  130.9 19.3 %collective-permute-start.25 = (bf16[4,160,640]{2,1,0:T(8,128)(2,1)S(1)}, bf16[4,160,640]{2,1,0:T(8,128)(2,1)S(1)}, u32[]{:S(2)}, u32[]{:S(2)}) collective-permute-start(bf16[4,160,640]{2,1,0:T(8,128)(2,1)S(1)} %pad_maximum_fusion.1.refs_0_.refs_1_), channel_id=1, source_target_pairs={{0,2},{2,0},{4,6},{6,4},{8,10},{10,8},{12,14},{14,12},{16,18},{18,... | collective-permute-start | bytes 2457608 | tf_op jit(solution)/shard_map/ppermute | solution.py:36
  174.4 20.3 %collective-permute-start.66 = (bf16[2,80,640]{2,1,0:T(8,128)(2,1)S(1)}, bf16[2,80,640]{2,1,0:T(8,128)(2,1)S(1)}, u32[]{:S(2)}, u32[]{:S(2)}) collective-permute-start(bf16[2,80,640]{2,1,0:T(8,128)(2,1)S(1)} %get-tuple-element.117), channel_id=1, source_target_pairs={{0,2},{2,0},{4,6},{6,4},{8,10},{10,8},{12,14},{14,12},{16,18},{18,... | collective-permute-start | bytes 614408 | tf_op jit(solution)/shard_map/ppermute | solution.py:36
  191.3 16.3 %collective-permute-start.57 = (bf16[2,80,640]{2,1,0:T(8,128)(2,1)S(1)}, bf16[2,80,640]{2,1,0:T(8,128)(2,1)S(1)}, u32[]{:S(2)}, u32[]{:S(2)}) collective-permute-start(bf16[2,80,640]{2,1,0:T(8,128)(2,1)S(1)} %get-tuple-element.110), channel_id=1, source_target_pairs={{0,4},{2,6},{4,0},{6,2},{8,12},{10,14},{12,8},{14,10},{16,20},{18,... | collective-permute-start | bytes 614408 | tf_op jit(solution)/shard_map/ppermute | solution.py:40
  195.5 23.5 %collective-permute-start.67 = (bf16[4,80,640]{2,1,0:T(8,128)(2,1)}, bf16[4,80,640]{2,1,0:T(8,128)(2,1)}, u32[]{:S(2)}, u32[]{:S(2)}) collective-permute-start(bf16[4,80,640]{2,1,0:T(8,128)(2,1)} %pad_maximum_fusion.10), channel_id=1, source_target_pairs={{0,4},{2,6},{4,0},{6,2},{8,12},{10,14},{12,8},{14,10},{16,20},{18,... | collective-permute-start | bytes 1228808 | tf_op jit(solution)/shard_map/ppermute | solution.py:40
  204.7 15.0 %collective-permute-start.65 = (bf16[4,80,640]{2,1,0:T(8,128)(2,1)}, bf16[4,80,640]{2,1,0:T(8,128)(2,1)}, u32[]{:S(2)}, u32[]{:S(2)}) collective-permute-start(bf16[4,80,640]{2,1,0:T(8,128)(2,1)} %pad_maximum_fusion.9), channel_id=1, source_target_pairs={{0,2},{2,0},{4,6},{6,4},{8,10},{10,8},{12,14},{14,12},{16,18},{18,... | collective-permute-start | bytes 1228808 | tf_op jit(solution)/shard_map/ppermute | solution.py:36
  210.0 36.5 %collective-permute-start.30 = (bf16[704,1280]{1,0:T(8,128)(2,1)}, bf16[704,1280]{1,0:T(8,128)(2,1)}, u32[]{:S(2)}, u32[]{:S(2)}) collective-permute-start(bf16[704,1280]{1,0:T(8,128)(2,1)} %get-tuple-element.79.mine), channel_id=1, source_target_pairs={{0,1},{1,0},{2,3},{3,2},{4,5},{5,4},{6,7},{7,6},{8,9},{9,8},{10,11... | collective-permute-start | bytes 5406728 | tf_op jit(solution)/shard_map/ppermute | solution.py:52
  219.1 138.9 %collective-permute-start.29 = (bf16[704,1280]{1,0:T(8,128)(2,1)S(1)}, bf16[704,1280]{1,0:T(8,128)(2,1)S(1)}, u32[]{:S(2)}, u32[]{:S(2)}) collective-permute-start(bf16[704,1280]{1,0:T(8,128)(2,1)S(1)} %mlp_down.1.mine), channel_id=1, source_target_pairs={{0,1},{1,0},{2,3},{3,2},{4,5},{5,4},{6,7},{7,6},{8,9},{9,8},{10,11... | collective-permute-start | bytes 5406728 | tf_op jit(solution)/shard_map/ppermute | solution.py:52
  239.3 118.7 %collective-permute-start.63 = (bf16[80,640]{1,0:T(8,128)(2,1)}, bf16[80,640]{1,0:T(8,128)(2,1)}, u32[]{:S(2)}, u32[]{:S(2)}) collective-permute-start(bf16[80,640]{1,0:T(8,128)(2,1)} %fusion.7), channel_id=1, source_target_pairs={{0,8},{2,10},{4,12},{6,14},{8,16},{10,18},{12,20},{14,22},{16,24},... | collective-permute-start | bytes 307208 | tf_op jit(solution)/shard_map/ppermute | solution.py:44
  267.4 48.0 %collective-permute-start.46 = (bf16[2,80,640]{2,1,0:T(8,128)(2,1)}, bf16[2,80,640]{2,1,0:T(8,128)(2,1)}, u32[]{:S(2)}, u32[]{:S(2)}) collective-permute-start(bf16[2,80,640]{2,1,0:T(8,128)(2,1)} %get-tuple-element.99), channel_id=1, source_target_pairs={{0,4},{2,6},{4,0},{6,2},{8,12},{10,14},{12,8},{14,10},{16,20},{18,... | collective-permute-start | bytes 614408 | tf_op jit(solution)/shard_map/ppermute | solution.py:40
  267.9 49.3 %collective-permute-start.48 = (bf16[2,80,640]{2,1,0:T(8,128)(2,1)}, bf16[2,80,640]{2,1,0:T(8,128)(2,1)}, u32[]{:S(2)}, u32[]{:S(2)}) collective-permute-start(bf16[2,80,640]{2,1,0:T(8,128)(2,1)} %get-tuple-element.101), channel_id=1, source_target_pairs={{0,2},{2,0},{4,6},{6,4},{8,10},{10,8},{12,14},{14,12},{16,18},{18,... | collective-permute-start | bytes 614408 | tf_op jit(solution)/shard_map/ppermute | solution.py:36
  300.1 31.7 %collective-permute-start.39 = (bf16[4,80,640]{2,1,0:T(8,128)(2,1)}, bf16[4,80,640]{2,1,0:T(8,128)(2,1)}, u32[]{:S(2)}, u32[]{:S(2)}) collective-permute-start(bf16[4,80,640]{2,1,0:T(8,128)(2,1)} %get-tuple-element.95), channel_id=1, source_target_pairs={{0,8},{2,10},{4,12},{6,14},{8,16},{10,18},{12,20},{14,22},{16,24},... | collective-permute-start | bytes 1228808 | tf_op jit(solution)/shard_map/ppermute | solution.py:44
  331.8 54.7 %collective-permute-start.31 = (bf16[704,1280]{1,0:T(8,128)(2,1)}, bf16[704,1280]{1,0:T(8,128)(2,1)}, u32[]{:S(2)}, u32[]{:S(2)}) collective-permute-start(bf16[704,1280]{1,0:T(8,128)(2,1)} %attention_in_back.1.mine), channel_id=1, source_target_pairs={{0,1},{1,0},{2,3},{3,2},{4,5},{5,4},{6,7},{7,6},{8,9},{9,8},{10,11... | collective-permute-start | bytes 5406728 | tf_op jit(solution)/shard_map/ppermute | solution.py:52
  348.9 23.8 %collective-permute-start.35 = (bf16[4,160,640]{2,1,0:T(8,128)(2,1)}, bf16[4,160,640]{2,1,0:T(8,128)(2,1)}, u32[]{:S(2)}, u32[]{:S(2)}) collective-permute-start(bf16[4,160,640]{2,1,0:T(8,128)(2,1)} %pad_maximum_fusion.3), channel_id=1, source_target_pairs={{0,4},{2,6},{4,0},{6,2},{8,12},{10,14},{12,8},{14,10},{16,20},{18,... | collective-permute-start | bytes 2457608 | tf_op jit(solution)/shard_map/ppermute | solution.py:40
  355.9 16.8 %collective-permute-start.33 = (bf16[4,160,640]{2,1,0:T(8,128)(2,1)}, bf16[4,160,640]{2,1,0:T(8,128)(2,1)}, u32[]{:S(2)}, u32[]{:S(2)}) collective-permute-start(bf16[4,160,640]{2,1,0:T(8,128)(2,1)} %pad_maximum_fusion.2), channel_id=1, source_target_pairs={{0,2},{2,0},{4,6},{6,4},{8,10},{10,8},{12,14},{14,12},{16,18},{18,... | collective-permute-start | bytes 2457608 | tf_op jit(solution)/shard_map/ppermute | solution.py:36
  (130 other events, 1719.0 us)
